TPU v7x, 32 devices: a whole 2x2x4 slice. The times are simulated.
32 devices in a mesh: dp: 8 (over z, x), mp: 4 (over y, core).
Axes of the slice: x: 2, y: 2, z: 4, core: 2. Of those that a mesh axis runs over, the one named last changes fastest.
Arguments:
- tokens: bfloat16 [8, 1024, 1024], P('dp', 'mp'), may hold values from -6 to 6
- seg_lengths: int32 [8, 2], P('dp'), may hold values from 1 to 896, 1024 in all within a row
- cotangent: bfloat16 [8, 1024, 1024], P('dp', 'mp'), may hold values from -6 to 6
- mixer_norm_gain: float32 [2, 1024], replicated, may hold values from 0.5 to 1.5
- mixer_norm_bias: float32 [2, 1024], replicated, may hold values from -3 to 3
- in_weight: bfloat16 [2, 1024, 3, 1024], P(None, None, None, 'mp'), may hold values from -0.1875 to 0.1875
- in_bias: float32 [2, 3, 1024], P(None, None, 'mp'), may hold values from -3 to 3
- conv_weight: float32 [2, 3, 3, 1024], P(None, None, None, 'mp'), may hold values from -3 to 3
- conv_bias: float32 [2, 3, 1024], P(None, None, 'mp'), may hold values from -3 to 3
- filter_in: float32 [2, 33, 64], replicated, may hold values from -1 to 1
- filter_in_bias: float32 [2, 64], replicated, may hold values from -4 to 4
- filter_in_freq: float32 [2, 64], replicated, may hold values from 0.1 to 1.9
- filter_mid: float32 [2, 64, 64], replicated, may hold values from -0.75 to 0.75
- filter_mid_bias: float32 [2, 64], replicated, may hold values from -4 to 4
- filter_mid_freq: float32 [2, 64], replicated, may hold values from 0.1 to 1.9
- filter_out: float32 [2, 64, 1024], P(None, None, 'mp'), may hold values from -0.09375 to 0.09375
- skip_bias: float32 [2, 1024], P(None, 'mp'), may hold values from -4 to 4
- out_weight: bfloat16 [2, 1024, 1024], P(None, 'mp'), may hold values from -0.1875 to 0.1875
- out_bias: float32 [2, 1024], replicated, may hold values from -3 to 3
- feed_norm_gain: float32 [2, 1024], replicated, may hold values from 0.5 to 1.5
- feed_norm_bias: float32 [2, 1024], replicated, may hold values from -3 to 3
- feed_up: bfloat16 [2, 1024, 4096], P(None, None, 'mp'), may hold values from -0.1875 to 0.1875
- feed_up_bias: float32 [2, 4096], P(None, 'mp'), may hold values from -3 to 3
- feed_down: bfloat16 [2, 4096, 1024], P(None, 'mp'), may hold values from -0.09375 to 0.09375
- feed_down_bias: float32 [2, 1024], replicated, may hold values from -3 to 3
Outputs:
- outputs: float32 [8, 1024, 1024], P('dp', 'mp')
- token_grad: float32 [8, 1024, 1024], P('dp', 'mp')
- mixer_norm_gain_grad: float32 [2, 1024], replicated
- mixer_norm_bias_grad: float32 [2, 1024], replicated
- in_weight_grad: float32 [2, 1024, 3, 1024], P(None, 'dp', None, 'mp')
- in_bias_grad: float32 [2, 3, 1024], P(None, None, 'mp')
- conv_weight_grad: float32 [2, 3, 3, 1024], P(None, None, None, 'mp')
- conv_bias_grad: float32 [2, 3, 1024], P(None, None, 'mp')
- filter_in_grad: float32 [2, 33, 64], replicated
- filter_in_bias_grad: float32 [2, 64], replicated
- filter_in_freq_grad: float32 [2, 64], replicated
- filter_mid_grad: float32 [2, 64, 64], replicated
- filter_mid_bias_grad: float32 [2, 64], replicated
- filter_mid_freq_grad: float32 [2, 64], replicated
- filter_out_grad: float32 [2, 64, 1024], P(None, None, 'mp')
- skip_bias_grad: float32 [2, 1024], P(None, 'mp')
- out_weight_grad: float32 [2, 1024, 1024], P(None, 'mp', 'dp')
- out_bias_grad: float32 [2, 1024], replicated
- feed_norm_gain_grad: float32 [2, 1024], replicated
- feed_norm_bias_grad: float32 [2, 1024], replicated
- feed_up_grad: float32 [2, 1024, 4096], P(None, 'dp', 'mp')
- feed_up_bias_grad: float32 [2, 4096], P(None, 'mp')
- feed_down_grad: float32 [2, 4096, 1024], P(None, 'mp', 'dp')
- feed_down_bias_grad: float32 [2, 1024], replicated
Inputs may be any that keep to these rules, and one draw needn't show every extreme that they name: `seg_lengths`: each row's 2 segment lengths sum to 1024; none is longer than 896.
All inputs are finite; a program needn't handle non-finite values.
Results may differ from a plain program's by a relative error of at most 0.023.
Values may be sent and summed in bfloat16 or wider, within the bound.
No kernel may reach another device: no remote copies, remote signals or barrier semaphores. Data moves between devices by JAX's collectives and lax.ppermute only.
A program may use at most 256 MiB of HBM per device.

v0:
```python
import functools
import math

import jax
import jax.numpy as jnp
import ml_dtypes
import numpy as np
from jax import lax
from jax.experimental import pallas as pl
from jax.experimental.pallas import tpu as pltpu
from jax.sharding import PartitionSpec as P

D = 1024
POS = 33
FILT = 64
REACH = 896
WAVES = 2 * REACH
SHORT = 3
STREAMS = 3
TILE = 128
CHUNK = 128
PARTS = D // CHUNK

f32 = jnp.float32
bf16 = jnp.bfloat16
highest = lax.Precision.HIGHEST
norm_eps = 1e-05
slow_rate = math.log(100.0) / 1.5
fast_rate = math.log(100.0) / 0.3
GELU_A = math.sqrt(2.0 / math.pi)
GELU_B = 0.044715
SPARE_MB = 3

ROW_IN_BIAS = 0
ROW_CONV_W = 3
ROW_CONV_B = 12
ROW_SKIP = 15
ROW_FILTER = 16
ROW_UP_BIAS = 80
ROW_WIDE = 84
ROW_NARROW = 116
PACK_ROWS = 144
NARROW_ROWS = 112
NARROW_GROUP = 28
NB_IN, NF_IN, NW_MID, NB_MID, NF_MID = 33, 34, 35, 99, 100


def wave_table(length):
    freq = 2 * np.arange(REACH, dtype=np.int64) + 1
    phase = (freq[:, None] * np.arange(length, dtype=np.int64)[None, :]) % (2 * WAVES)
    angle = phase.astype(np.float64) * (math.pi / WAVES)
    return np.concatenate([np.cos(angle), -np.sin(angle)], axis=0).astype(ml_dtypes.bfloat16)


def position_table(length):
    places = np.arange(REACH, dtype=np.float64)
    count = (POS - 1) // 2
    bands = 0.0001 + np.arange(count, dtype=np.float64) * ((count - 1 - 0.0001) / (count - 1))
    phases = bands[:, None] * places[None, :] * (2.0 * math.pi / length)
    table = np.zeros((64, REACH), np.float32)
    table[0] = places / (length - 1)
    table[1 : 1 + count] = np.cos(phases)
    table[1 + count : POS] = -np.sin(phases)
    return table


def core_swap(x):
    size = lax.axis_size("mp")
    return lax.ppermute(x, "mp", [(i, i ^ 1) for i in range(size)])


def chip_swap(x):
    size = lax.axis_size("mp")
    return lax.ppermute(x, "mp", [(i, i ^ 2) for i in range(size)])


def dot(a, b):
    return jnp.dot(a, b, preferred_element_type=f32)


def dot_rows(a, b):
    return lax.dot_general(a, b, (((0,), (0,)), ((), ())), preferred_element_type=f32)


def dot_cols(a, b):
    return lax.dot_general(a, b, (((1,), (1,)), ((), ())), preferred_element_type=f32)


def fine(a, b, dims):
    return lax.dot_general(a, b, (dims, ((), ())), precision=highest, preferred_element_type=f32)


def whole(shape):
    return pl.BlockSpec(tuple(shape), lambda *_: (0,) * len(shape))


def layer_of(stacked, layer):
    shape = stacked.shape[1:]
    return pl.BlockSpec((None, *shape), lambda *_: (layer,) + (0,) * len(shape))


SMALL = pl.BlockSpec(memory_space=pltpu.SMEM)
FAR = pl.BlockSpec(memory_space=pl.ANY)
MAIN = pl.BlockSpec(memory_space=pltpu.HBM)


def struct(shape, dtype):
    return jax.ShapeDtypeStruct(tuple(shape), dtype)


class Chain:
    def __init__(self):
        self.token = None

    def release(self, arrays):
        *results, self.token = pl.pallas_call(
            lambda *refs: None,
            grid=(1,),
            out_shape=[pltpu.HBM(a.shape, a.dtype) for a in arrays] + [pltpu.HBM((8, 128), f32)],
            in_specs=[FAR] * (len(arrays) + 1),
            out_specs=[MAIN] * (len(arrays) + 1),
            input_output_aliases={i: i for i in range(len(arrays))},
            cost_estimate=pl.CostEstimate(flops=1, bytes_accessed=1, transcendentals=0),
            name="release",
        )(*[stay(a) for a in arrays], stay(self.token))
        return results

    def __call__(self, kernel, operands, outs, scratch=(), far=0, spill=0, name=None, after=()):
        arrays = [a for a, _ in operands]
        specs = [whole(a.shape) if s is None else s for a, s in operands]
        main = far + spill
        out_specs = [MAIN if i < main else whole(o.shape) for i, o in enumerate(outs)]
        spilled = [pltpu.VMEM(o.shape, o.dtype) for o in outs[far:main]]
        scratch = [*scratch, *spilled] + ([pltpu.SemaphoreType.DMA((spill,))] if spill else [])
        held = 0
        for a, s in list(zip(arrays, specs)) + list(zip(outs, out_specs)):
            if s is not SMALL and s is not FAR and s is not MAIN:
                held += math.prod(x for x in s.block_shape if x is not None) * a.dtype.itemsize
        for s in scratch:
            if getattr(s, "memory_space", None) == pltpu.VMEM:
                held += math.prod(s.shape) * jnp.dtype(s.dtype).itemsize
        count, given = len(arrays), len(outs)
        tokens = ([] if self.token is None else [stay(self.token)]) + list(after)

        def body(*refs):
            ins, refs = refs[:count], refs[count + len(tokens) :]
            results, rest = refs[:given], refs[given + 1 :]
            if spill:
                rest, buffers, sems = rest[: -spill - 1], rest[-spill - 1 : -1], rest[-1]
                kernel(*ins, *results[:far], *buffers, *results[main:], *rest)
                copies = [
                    pltpu.make_async_copy(buffers[i], results[far + i], sems.at[i]) for i in range(spill)
                ]
                for copy in copies:
                    copy.start()
                for copy in copies:
                    copy.wait()
            else:
                kernel(*ins, *results, *rest)

        *results, self.token = pl.pallas_call(
            body,
            grid=(1,),
            out_shape=[pltpu.HBM(o.shape, o.dtype) if i < main else o for i, o in enumerate(outs)]
            + [pltpu.HBM((8, 128), f32)],
            in_specs=specs + [FAR] * len(tokens),
            out_specs=out_specs + [MAIN],
            scratch_shapes=scratch,
            compiler_params=pltpu.CompilerParams(vmem_limit_bytes=held + SPARE_MB * 1024 * 1024),
            cost_estimate=pl.CostEstimate(flops=1, bytes_accessed=1, transcendentals=0),
            name=name,
        )(*arrays, *tokens)
        return results


def unit_of(values):
    center = values - jnp.mean(values, axis=-1, keepdims=True)
    spread = jnp.mean(center * center, axis=-1, keepdims=True)
    rstd = lax.rsqrt(spread + norm_eps)
    return center * rstd, rstd


def row_tiles(count, size=32):
    return [slice(i * size, (i + 1) * size) for i in range(count // size)]


def stay(x):
    return pltpu.with_memory_space_constraint(x, pltpu.HBM)


def first_norm_kernel(scal, mine, other, gain, shift, cot, low_a, low_b, res_a, res_b, cot_out):
    chip = scal[2]
    cot_out[...] = cot[...]
    for rows in row_tiles(mine.shape[0]):
        a, b = mine[rows, :].astype(f32), other[rows, :].astype(f32)
        for values, res, low in (
            (jnp.where(chip == 0, a, b), res_a, low_a),
            (jnp.where(chip == 0, b, a), res_b, low_b),
        ):
            res[rows, :] = values
            unit, _ = unit_of(values)
            low[rows, :] = (unit * gain[0:1, :] + shift[0:1, :]).astype(bf16)


def first_norm(run, scal, mine, other, gain, shift, cot):
    block = mine.shape[0]
    return run(
        first_norm_kernel,
        [(scal, SMALL)] + [(a, None) for a in (mine, other, gain, shift, cot)],
        [struct((block, D), bf16)] * 2 + [struct((block, D), f32)] * 2 + [struct((block, D), bf16)],
        spill=2,
        name="first_norm",
    )


def first_grad_kernel(scal, mine, other, sums, low_a, low_b):
    chip = scal[2]
    total = jnp.zeros((8, D), f32)
    for rows in row_tiles(mine.shape[0]):
        a, b = mine[rows, :], other[rows, :]
        low_a[rows, :] = jnp.where(chip == 0, a, b)
        low_b[rows, :] = jnp.where(chip == 0, b, a)
        total = total + fold(a.astype(f32)) + fold(b.astype(f32))
    sums[...] = 0.5 * jnp.sum(total, axis=0, keepdims=True)


def first_grad(run, scal, mine, other):
    block = mine.shape[0]
    return run(
        first_grad_kernel,
        [(scal, SMALL), (mine, None), (other, None)],
        [struct((1, D), f32)] + [struct((block, D), bf16)] * 2,
        spill=1,
        name="first_grad",
    )


def add_kernel(keep, got, out):
    for rows in row_tiles(keep.shape[0], 64):
        out[rows, :] = (keep[rows, :] + got[rows, :].astype(f32)).astype(out.dtype)


def add_low(run, keep, got, after=()):
    out = [struct(keep.shape, bf16)]
    return run(add_kernel, [(keep, None), (got, None)], out, name="add_low", after=after)[0]


def last_pick_kernel(scal, keep_a, got_a, val_a, keep_b, got_b, val_b, send, mine, sums):
    totals = [jnp.zeros((8, D), f32) for _ in range(2)]
    near_a = scal[2] == 0
    for rows in row_tiles(mine.shape[0]):
        parts = []
        for keep, got, values in ((keep_a, got_a, val_a), (keep_b, got_b, val_b)):
            total = keep[rows, :] + got[rows, :].astype(f32)
            unit, _ = unit_of(values[rows, :])
            totals[0] = totals[0] + fold(total * unit)
            totals[1] = totals[1] + fold(total)
            parts.append(total)
        mine[rows, :] = jnp.where(near_a, parts[0], parts[1])
        send[rows, :] = jnp.where(near_a, parts[1], parts[0]).astype(bf16)
    for i, total in enumerate(totals):
        sums[i : i + 1, :] = jnp.sum(total, axis=0, keepdims=True)
    sums[2:8, :] = jnp.zeros((6, D), f32)


def last_pick(run, scal, keeps, gots, entry):
    shape = keeps[0].shape
    operands = [a for i in range(2) for a in (keeps[i], gots[i], entry[i])]
    return run(
        last_pick_kernel,
        [(scal, SMALL)] + [(a, None) for a in operands],
        [struct(shape, bf16), struct(shape, f32), struct((8, D), f32)],
        name="last_pick",
    )


def add_norm_kernel(layer, norm_layer, here, there, residual, bias, gain, shift, low, out):
    for rows in row_tiles(here.shape[0]):
        values = residual[rows, :] + here[rows, :].astype(f32) + there[rows, :].astype(f32)
        values = values + bias[layer : layer + 1, :]
        out[rows, :] = values
        unit, _ = unit_of(values)
        low[rows, :] = (
            unit * gain[norm_layer : norm_layer + 1, :] + shift[norm_layer : norm_layer + 1, :]
        ).astype(bf16)


def add_norm(run, layer, norm_layer, here, there, residual, bias, gain, shift, spill=0):
    shape = here.shape
    return run(
        functools.partial(add_norm_kernel, layer, norm_layer),
        [(a, None) for a in (here, there, residual, bias, gain, shift)],
        [struct(shape, bf16), struct(shape, f32)],
        spill=spill,
        name="add_norm",
    )


def pick_kernel(layer, scal, keep_a, got_a, keep_b, got_b, mid_a, mid_b, bias, send, mine):
    def pick(near, far_away):
        keep, got, middle = near
        for rows in row_tiles(mine.shape[0]):
            values = keep[rows, :] + got[rows, :].astype(f32) + middle[rows, :]
            mine[rows, :] = values + bias[layer : layer + 1, :]
            send[rows, :] = (far_away[0][rows, :] + far_away[1][rows, :].astype(f32)).astype(bf16)

    @pl.when(scal[2] == 0)
    def _():
        pick((keep_a, got_a, mid_a), (keep_b, got_b))

    @pl.when(scal[2] != 0)
    def _():
        pick((keep_b, got_b, mid_b), (keep_a, got_a))


def pick_outputs(run, layer, scal, keeps, gots, middles, bias):
    shape = keeps[0].shape
    operands = (keeps[0], gots[0], keeps[1], gots[1], *middles, bias)
    return run(
        functools.partial(pick_kernel, layer),
        [(scal, SMALL)] + [(a, None) for a in operands],
        [struct(shape, bf16), struct(shape, f32)],
        name="pick_outputs",
    )


def last_add_kernel(mine, there, out):
    for rows in row_tiles(out.shape[0], 64):
        out[rows, :] = mine[rows, :] + there[rows, :].astype(f32)


def last_add(run, mine, there):
    return run(last_add_kernel, [(mine, None), (there, None)], [struct(mine.shape, f32)], name="last_add")[0]


def fold(x):
    return sum(x[8 * i : 8 * i + 8, :] for i in range(x.shape[0] // 8))


def norm_back_kernel(layer, here, there, values, grad, gain, out, sums, low):
    totals = [jnp.zeros((8, D), f32) for _ in range(3)]
    for rows in row_tiles(here.shape[0], 16):
        dy = here[rows, :].astype(f32) + there[rows, :].astype(f32)
        unit, rstd = unit_of(values[rows, :])
        scaled = dy * gain[layer : layer + 1, :]
        into = rstd * (
            scaled
            - jnp.mean(scaled, axis=-1, keepdims=True)
            - unit * jnp.mean(scaled * unit, axis=-1, keepdims=True)
        )
        new = grad[rows, :].astype(f32) + into
        out[rows, :] = new
        low[rows, :] = new.astype(bf16)
        for k, part in enumerate((dy * unit, dy, new)):
            totals[k] = totals[k] + fold(part)
    for k, total in enumerate(totals):
        sums[k : k + 1, :] = 0.5 * jnp.sum(total, axis=0, keepdims=True)
    sums[3:8, :] = jnp.zeros((5, D), f32)


def norm_back(run, layer, here, there, values, grad, gain, spill=0):
    shape = here.shape
    return run(
        functools.partial(norm_back_kernel, layer),
        [(a, None) for a in (here, there, values, grad, gain)],
        [struct(shape, f32), struct((8, D), f32), struct(shape, bf16)],
        spill=2 + spill,
        name="norm_back",
    )


def last_back_kernel(layer, scal, mine, there, val_a, val_b, grad_a, grad_b, gain, out):
    near_a = scal[2] == 0
    for rows in row_tiles(out.shape[0], 16):
        dy = mine[rows, :] + there[rows, :].astype(f32)
        unit, rstd = unit_of(jnp.where(near_a, val_a[rows, :], val_b[rows, :]))
        scaled = dy * gain[layer : layer + 1, :]
        into = rstd * (
            scaled
            - jnp.mean(scaled, axis=-1, keepdims=True)
            - unit * jnp.mean(scaled * unit, axis=-1, keepdims=True)
        )
        out[rows, :] = jnp.where(near_a, grad_a[rows, :], grad_b[rows, :]) + into


def last_back(run, layer, scal, mine, there, entry, grad, gain):
    return run(
        functools.partial(last_back_kernel, layer),
        [(scal, SMALL), (mine, None), (there, None)]
        + [(a, None) for a in (*entry, *grad, gain)],
        [struct(mine.shape, f32)],
        name="last_back",
    )[0]


def ffn_fwd_kernel(
    layer, own, got, up_far, up_bias, down_far, pre_far, hid_far, sent, keep, both, pre, hid, up, down, sems
):
    copy_up = pltpu.make_async_copy(up_far.at[layer], up, sems.at[2])
    copy_down = pltpu.make_async_copy(down_far.at[layer], down, sems.at[3])
    copy_up.start()
    copy_down.start()
    half = own.shape[0]
    both[:half, :] = own[...]
    both[half:, :] = got[...]
    copy_up.wait()
    v = dot(both[...], up[...]) + up_bias[layer : layer + 1, :]
    pre[...] = v.astype(bf16)
    hid[...] = (0.5 * v * (1.0 + jnp.tanh(GELU_A * (v + GELU_B * v * v * v)))).astype(bf16)
    copies = [
        pltpu.make_async_copy(a, b, sems.at[i]) for i, (a, b) in enumerate(((pre, pre_far), (hid, hid_far)))
    ]
    for copy in copies:
        copy.start()
    copy_down.wait()
    total = dot(hid[...], down[...])
    keep[...] = total[:half, :]
    sent[...] = total[half:, :].astype(bf16)
    for copy in copies:
        copy.wait()


def ffn_fwd(run, layer, own, got, up, up_bias, down):
    half, width = own.shape[0], up.shape[2]
    return run(
        functools.partial(ffn_fwd_kernel, layer),
        [(own, None), (got, None), (up, FAR), (up_bias, None), (down, FAR)],
        [
            struct((2 * half, width), bf16),
            struct((2 * half, width), bf16),
            struct((half, D), bf16),
            struct((half, D), f32),
        ],
        scratch=[
            pltpu.VMEM((2 * half, D), bf16),
            pltpu.VMEM((2 * half, width), bf16),
            pltpu.VMEM((2 * half, width), bf16),
            pltpu.VMEM((D, width), bf16),
            pltpu.VMEM((width, D), bf16),
            pltpu.SemaphoreType.DMA((4,)),
        ],
        far=2,
        name="ffn_fwd",
    )


def ffn_bwd_kernel(
    layer, own, got, up_far, down_far, pre_far, up_low_far, bias_sum, sent, keep,
    both, up, down, pre, up_low, sems,
):
    ins = ((down_far.at[layer], down), (pre_far, pre), (up_far.at[layer], up))
    copies = [pltpu.make_async_copy(a, b, sems.at[i]) for i, (a, b) in enumerate(ins)]
    for copy in copies:
        copy.start()
    half = own.shape[0]
    both[:half, :] = own[...]
    both[half:, :] = got[...]
    copies[0].wait()
    copies[1].wait()
    v = pre[...].astype(f32)
    t = jnp.tanh(GELU_A * (v + GELU_B * v * v * v))
    slope = 0.5 * (1.0 + t) + 0.5 * v * (1.0 - t * t) * (GELU_A * (1.0 + 3.0 * GELU_B * v * v))
    g = dot_cols(both[...], down[...]) * slope
    bias_sum[...] = jnp.sum(g, axis=0, keepdims=True)
    up_low[...] = g.astype(bf16)
    copy_low = pltpu.make_async_copy(up_low, up_low_far, sems.at[3])
    copy_low.start()
    copies[2].wait()
    total = dot_cols(up_low[...], up[...])
    keep[...] = total[:half, :]
    sent[...] = total[half:, :].astype(bf16)
    copy_low.wait()


def ffn_bwd(run, layer, own, got, up, down, pre, near):
    half, width = own.shape[0], up.shape[2]
    if not near:
        up, down = stay(up), stay(down)
    up_low, bias_sum, sent, keep = run(
        functools.partial(ffn_bwd_kernel, layer),
        [(own, None), (got, None), (up, FAR), (down, FAR), (stay(pre), FAR)],
        [
            struct((2 * half, width), bf16),
            struct((1, width), f32),
            struct((half, D), bf16),
            struct((half, D), f32),
        ],
        scratch=[
            pltpu.VMEM((2 * half, D), bf16),
            pltpu.VMEM((D, width), bf16),
            pltpu.VMEM((width, D), bf16),
            pltpu.VMEM((2 * half, width), bf16),
            pltpu.VMEM((2 * half, width), bf16),
            pltpu.SemaphoreType.DMA((4,)),
        ],
        far=1,
        spill=1,
        name="ffn_bwd",
    )
    return bias_sum, up_low, sent, keep


def sine(x, both=False):
    turns = jnp.floor(x * (1.0 / math.pi) + 0.5)
    rest = (x - turns * 3.140625) - turns * 9.67653589793e-4
    sign = 1.0 - 2.0 * (turns - 2.0 * jnp.floor(turns * 0.5))
    sq = rest * rest
    odd = -1.0 / 39916800.0
    for c in (1.0 / 362880.0, -1.0 / 5040.0, 1.0 / 120.0, -1.0 / 6.0, 1.0):
        odd = odd * sq + c
    value = sign * rest * odd
    if not both:
        return value
    even = 1.0 / 479001600.0
    for c in (-1.0 / 3628800.0, 1.0 / 40320.0, -1.0 / 720.0, 1.0 / 24.0, -0.5, 1.0):
        even = even * sq + c
    return value, sign * even


def decay(spot, channels, length):
    lane = lax.broadcasted_iota(jnp.int32, (1, channels), 1) + spot * channels
    row = lax.broadcasted_iota(jnp.int32, (REACH, channels), 0).astype(f32)
    rate = slow_rate + (fast_rate - slow_rate) * lane.astype(f32) / (D - 1)
    return jnp.exp(-(row * (1.0 / (length - 1))) * rate)


def columns(layer, *refs):
    rows = [r[layer : layer + 1, :] for r in refs] + [jnp.zeros((8 - len(refs), FILT), f32)]
    wide = jnp.concatenate([jnp.concatenate(rows, axis=0), jnp.zeros((8, 128 - FILT), f32)], axis=1).T
    return [wide[:FILT, i : i + 1] for i in range(len(refs))]


def filter_fwd_kernel(
    layer, length, scal, pos, w_in, b_in, f_in, w_mid, b_mid, f_mid, w_out, waves, spec, kept
):
    channels = w_out.shape[1]
    b_in, f_in, b_mid, f_mid = columns(layer, b_in, f_in, b_mid, f_mid)
    z = fine(w_in[...], pos[:POS, :], ((0,), (0,))) + b_in
    h, c = sine(f_in * z, both=True)
    kept[0] = z
    kept[1] = h
    kept[2] = c
    z = fine(w_mid[...], h, ((0,), (0,))) + b_mid
    h, c = sine(f_mid * z, both=True)
    kept[3] = z
    kept[4] = h
    kept[5] = c
    taps = fine(h, w_out[...], ((0,), (0,))) * decay(scal[4], channels, length)
    spec[...] = dot(waves[:, :REACH], taps.astype(bf16)) * (2.0 / WAVES)


def filter_fwd(run, layer, length, scal, pos, weights, waves):
    channels = weights[-1].shape[2]
    return run(
        functools.partial(filter_fwd_kernel, layer, length),
        [(scal, SMALL), (pos, None)]
        + [(a, layer_of(a, layer) if a.ndim == 3 else None) for a in weights]
        + [(waves, None)],
        [struct((WAVES, channels), f32), struct((6, FILT, REACH), f32)],
        spill=2,
        name="filter_fwd",
    )


def filter_bwd_kernel(layer, length, scal, taps_grad, pos, f_in, w_mid, f_mid, w_out, kept, by_chan, narrow):
    channels = w_out.shape[1]
    dt = taps_grad[...] * decay(scal[4], channels, length)
    by_chan[...] = fine(kept[4], dt, ((1,), (0,)))
    f_in, f_mid = columns(layer, f_in, f_mid)
    dh = fine(w_out[...], dt, ((1,), (1,)))
    c = kept[5] * dh
    dz = c * f_mid
    narrow[NW_MID : NW_MID + FILT, :] = fine(kept[1], dz, ((1,), (1,)))
    mid_sums = jnp.concatenate(
        [jnp.sum(dz, axis=1, keepdims=True), jnp.sum(c * kept[3], axis=1, keepdims=True)], axis=1
    )
    dh = fine(w_mid[...], dz, ((1,), (0,)))
    c = kept[2] * dh
    dz = c * f_in
    narrow[:POS, :] = fine(pos[...], dz, ((1,), (1,)))[:POS, :]
    in_sums = jnp.concatenate(
        [jnp.sum(dz, axis=1, keepdims=True), jnp.sum(c * kept[0], axis=1, keepdims=True)], axis=1
    )
    sums = jnp.concatenate([in_sums, mid_sums, jnp.zeros((FILT, 124), f32)], axis=1).T
    narrow[NB_IN : NB_IN + 2, :] = sums[0:2, :]
    narrow[NB_MID : NB_MID + 2, :] = sums[2:4, :]
    narrow[NF_MID + 1 :, :] = jnp.zeros((NARROW_ROWS - NF_MID - 1, FILT), f32)


def filter_bwd(run, layer, length, scal, taps_grad, pos, weights, kept):
    _, _, f_in, w_mid, _, f_mid, w_out = weights
    return run(
        functools.partial(filter_bwd_kernel, layer, length),
        [(scal, SMALL), (taps_grad, None), (pos, None)]
        + [(a, layer_of(a, layer) if a.ndim == 3 else None) for a in (f_in, w_mid, f_mid, w_out)]
        + [(kept, None)],
        [struct((FILT, w_out.shape[2]), f32), struct((NARROW_ROWS, FILT), f32)],
        name="filter_bwd",
    )


def lagged(ref, tile, cols, lag, before=None):
    if tile:
        return ref[tile * TILE - lag : (tile + 1) * TILE - lag, cols]
    if before is None:
        head = jnp.zeros((lag, cols.stop - cols.start), f32)
    else:
        head = before[before.shape[0] - lag :, cols]
    return jnp.concatenate([head, ref[: TILE - lag, cols]], axis=0)


def ahead(ref, tile, cols, lag, last):
    if tile < last:
        return ref[tile * TILE + lag : (tile + 1) * TILE + lag, cols]
    empty = jnp.zeros((lag, cols.stop - cols.start), f32)
    return jnp.concatenate([ref[tile * TILE + lag : (tile + 1) * TILE, cols], empty], axis=0)


def place(tile, first, shift=0):
    row = lax.broadcasted_iota(jnp.int32, (TILE, 1), 0) + (tile * TILE + shift)
    in_first = row < first
    return in_first, jnp.where(in_first, row, row - first)


def short_tile(proj, conv_w, conv_b, layer, tile, stream, offset, channels, before=None):
    cols = slice(stream * channels, (stream + 1) * channels)
    row = slice(layer, layer + 1)
    total = proj[tile * TILE : (tile + 1) * TILE, cols] * conv_w[stream, 0, row, :]
    total = total + conv_b[stream, row, :]
    for lag in range(1, SHORT):
        weight = conv_w[stream, lag, row, :]
        total = total + jnp.where(offset >= lag, lagged(proj, tile, cols, lag, before) * weight, 0.0)
    return total


def tile_rows(tile):
    return slice(tile * TILE, (tile + 1) * TILE)


def halves(own_a, own_b, got_a, got_b, core):
    block = own_a.shape[0]
    out = []
    for half, (own, got) in enumerate(((own_a, got_a), (own_b, got_b))):
        for rows, side in ((own, core), (got, 1 - core)):
            out.append((rows, pl.multiple_of(2 * block * half + side * block, block)))
    return out


def mix_fwd_kernel(layer, half, *refs):
    (scal, in_b, conv_w, conv_b, skip, own_far, got_far, in_w_far, taps_far, out_w_far, waves_far, waves_t_far), refs = (
        refs[:12],
        refs[12:],
    )
    before, prev = None, None
    if half:
        (before, prev), refs = refs[:2], refs[2:]
    (proj_far, longc_far, mixed_far, spec, tail, sent, keep), refs = refs[:7], refs[7:]
    own, got, in_w, waves, waves_t, taps, out_w, proj, gated, mixed, s0, pieces, prod, sems = refs
    block = own.shape[0]
    length = 2 * block
    first_ins = ((own_far, own), (got_far, got), (in_w_far.at[layer], in_w))
    first_copies = [pltpu.make_async_copy(a, b, sems.at[8 + i]) for i, (a, b) in enumerate(first_ins)]
    for copy in first_copies:
        copy.start()
    places = slice(half * length, (half + 1) * length)
    ins = [
        (waves_far.at[:, places], waves),
        (taps_far, taps),
        (waves_t_far.at[places, :], waves_t),
        (out_w_far.at[layer], out_w),
    ]
    copies = [pltpu.make_async_copy(a, b, sems.at[i]) for i, (a, b) in enumerate(ins)]
    outs = ((proj, proj_far), (gated, longc_far), (mixed, mixed_far))
    copy_proj, copy_long, copy_mixed = [
        pltpu.make_async_copy(a, b, sems.at[4 + i]) for i, (a, b) in enumerate(outs)
    ]
    for copy in copies:
        copy.start()
    for copy in first_copies:
        copy.wait()
    first, core = scal[0], scal[1]
    channels = skip.shape[1]
    row = slice(layer, layer + 1)
    sides = [pl.multiple_of(side * block, block) for side in (core, 1 - core)]
    for rows, at in zip((own, got), sides):
        for stream in range(STREAMS):
            cols = slice(stream * channels, (stream + 1) * channels)
            proj[pl.ds(at, block), cols] = dot(rows[...], in_w[stream]) + in_b[stream, row, :]
    copy_proj.start()
    tail[...] = proj[length - 8 :, :]
    for tile in range(length // TILE):
        rows = tile_rows(tile)
        in_first, offset = place(tile, first, half * length)
        one, two, zero = [
            short_tile(proj, conv_w, conv_b, layer, tile, stream, offset, channels, before)
            for stream in (1, 2, 0)
        ]
        g = one * two
        gated[rows, :] = g
        s0[rows, :] = zero
        pieces[rows, :channels] = jnp.where(in_first, g, 0.0).astype(bf16)
        pieces[rows, channels:] = jnp.where(in_first, 0.0, g).astype(bf16)
    copies[0].wait()
    copies[1].wait()
    steps = 2
    part = REACH // steps
    for step in range(steps):
        lo = slice(step * part, (step + 1) * part)
        hi = slice(REACH + step * part, REACH + (step + 1) * part)
        for seg in range(2):
            cols = slice(seg * channels, (seg + 1) * channels)
            re = dot(waves[lo, :], pieces[:, cols])
            im = dot(waves[hi, :], pieces[:, cols])
            if half:
                re = re + prev[lo, cols].astype(f32)
                im = im + prev[hi, cols].astype(f32)
            t_re, t_im = taps[lo, :], taps[hi, :]
            spec[lo, cols] = re.astype(bf16)
            spec[hi, cols] = im.astype(bf16)
            prod[lo, cols] = (re * t_re - im * t_im).astype(bf16)
            prod[hi, cols] = (re * t_im + im * t_re).astype(bf16)
    copies[2].wait()
    in_first = lax.broadcasted_iota(jnp.int32, (length, 1), 0) + half * length < first
    a = dot(waves_t[...], prod[:, :channels])
    b = dot(waves_t[...], prod[:, channels:])
    total = jnp.where(in_first, a, b) + skip[row, :] * gated[...]
    gated[...] = total
    mixed[...] = (total * s0[...]).astype(bf16)
    copy_long.start()
    copy_mixed.start()
    copies[3].wait()
    keep[...] = dot(mixed[pl.ds(sides[0], block), :], out_w[...])
    sent[...] = dot(mixed[pl.ds(sides[1], block), :], out_w[...]).astype(bf16)
    for copy in (copy_proj, copy_long, copy_mixed):
        copy.wait()


def mix_fwd(run, layer, half, scal, own, got, in_w, in_b, conv_w, conv_b, skip, taps, out_w, waves, waves_t, prev):
    block, channels = own.shape[0], skip.shape[1]
    length = 2 * block
    extra = [] if prev is None else [(a, None) for a in prev]
    proj, longc, mixed, spec, tail, sent, keep = run(
        functools.partial(mix_fwd_kernel, layer, half),
        [(scal, SMALL)]
        + [(a, None) for a in (in_b, conv_w, conv_b, skip)]
        + [(stay(own), FAR), (got, FAR)]
        + [(stay(a), FAR) for a in (in_w, taps, out_w, waves, waves_t)]
        + extra,
        [
            struct((length, STREAMS * channels), f32),
            struct((length, channels), f32),
            struct((length, channels), bf16),
            struct((WAVES, 2 * channels), bf16),
            struct((8, STREAMS * channels), f32),
            struct((block, D), bf16),
            struct((block, D), f32),
        ],
        scratch=[
            pltpu.VMEM((block, D), bf16),
            pltpu.VMEM((block, D), bf16),
            pltpu.VMEM((STREAMS, D, channels), bf16),
            pltpu.VMEM((WAVES, length), bf16),
            pltpu.VMEM((length, WAVES), bf16),
            pltpu.VMEM((WAVES, channels), f32),
            pltpu.VMEM((channels, D), bf16),
            pltpu.VMEM((length, STREAMS * channels), f32),
            pltpu.VMEM((length, channels), f32),
            pltpu.VMEM((length, channels), bf16),
            pltpu.VMEM((length, channels), f32),
            pltpu.VMEM((length, 2 * channels), bf16),
            pltpu.VMEM((WAVES, 2 * channels), bf16),
            pltpu.SemaphoreType.DMA((11,)),
        ],
        far=3,
        spill=half,
        name="mix_fwd",
    )
    return (proj, longc, mixed), (tail, spec), sent, keep


def mix_bwd_kernel(
    layer, scal, conv_w, conv_b, skip, own_a_far, own_b_far, got_a_far, got_b_far, out_w_far,
    proj_a_far, proj_b_far, longc_a_far, longc_b_far, waves_far, spec_far, taps_far, waves_t_far, in_w_far,
    in_low, taps_grad, sums, sent_a, sent_b, keep_a, keep_b,
    own_a, own_b, got_a, got_b, out_w, proj, longc, waves, spec, taps, waves_t, in_w, mgrad, ds, pieces, prod,
    corr, sems,
):
    first_ins = (
        (own_a_far, own_a),
        (own_b_far, own_b),
        (got_a_far, got_a),
        (got_b_far, got_b),
        (out_w_far.at[layer], out_w),
    )
    first_copies = [pltpu.make_async_copy(a, b, sems.at[9 + i]) for i, (a, b) in enumerate(first_ins)]
    for copy in first_copies:
        copy.start()
    half_rows = proj_a_far.shape[0]
    near, later = pl.ds(0, half_rows), pl.ds(half_rows, half_rows)
    ins = (
        (proj_a_far, proj.at[near, :]),
        (longc_a_far, longc.at[near, :]),
        (proj_b_far, proj.at[later, :]),
        (longc_b_far, longc.at[later, :]),
        (waves_far, waves),
        (spec_far, spec),
        (taps_far, taps),
        (waves_t_far, waves_t),
        (in_w_far.at[layer], in_w),
    )
    copies = [pltpu.make_async_copy(a, b, sems.at[i]) for i, (a, b) in enumerate(ins)]
    for copy in copies[:4]:
        copy.start()
    first, core = scal[0], scal[1]
    block = own_a.shape[0]
    channels = skip.shape[1]
    row = slice(layer, layer + 1)
    length = 4 * block
    tiles = length // TILE
    for copy in first_copies:
        copy.wait()
    for copy in copies[4:]:
        copy.start()
    for rows, at in halves(own_a, own_b, got_a, got_b, core):
        mgrad[pl.ds(at, block), :] = dot_cols(rows[...], out_w[...])
    skip_sum = jnp.zeros((1, channels), f32)
    for copy in copies[:4]:
        copy.wait()
    mid, end = slice(channels, 2 * channels), slice(2 * channels, 3 * channels)
    for tile in range(tiles):
        rows = tile_rows(tile)
        in_first, offset = place(tile, first)
        one = short_tile(proj, conv_w, conv_b, layer, tile, 1, offset, channels)
        two = short_tile(proj, conv_w, conv_b, layer, tile, 2, offset, channels)
        ds[rows, mid] = one
        ds[rows, end] = two
        m = mgrad[rows, :]
        r = m * short_tile(proj, conv_w, conv_b, layer, tile, 0, offset, channels)
        mgrad[rows, :] = r
        ds[rows, :channels] = m * longc[rows, :]
        skip_sum = skip_sum + jnp.sum(r * one * two, axis=0, keepdims=True)
        pieces[rows, :channels] = jnp.where(in_first, r, 0.0).astype(bf16)
        pieces[rows, channels:] = jnp.where(in_first, 0.0, r).astype(bf16)
    sums[ROW_SKIP : ROW_SKIP + 1, :] = skip_sum
    for copy in copies[4:7]:
        copy.wait()
    steps = 2
    part = REACH // steps
    for step in range(steps):
        lo = slice(step * part, (step + 1) * part)
        hi = slice(REACH + step * part, REACH + (step + 1) * part)
        corr_re, corr_im = None, None
        for seg in range(2):
            cols = slice(seg * channels, (seg + 1) * channels)
            re = dot(waves[lo, :], pieces[:, cols])
            im = dot(waves[hi, :], pieces[:, cols])
            t_re, t_im = taps[lo, :], taps[hi, :]
            prod[lo, cols] = (re * t_re + im * t_im).astype(bf16)
            prod[hi, cols] = (im * t_re - re * t_im).astype(bf16)
            g_re, g_im = spec[lo, cols].astype(f32), spec[hi, cols].astype(f32)
            c_re = g_re * re + g_im * im
            c_im = g_re * im - g_im * re
            corr_re = c_re if corr_re is None else corr_re + c_re
            corr_im = c_im if corr_im is None else corr_im + c_im
        corr[lo, :] = corr_re.astype(bf16)
        corr[hi, :] = corr_im.astype(bf16)
    copies[7].wait()
    big = 512
    for r in range(length // big):
        rows = slice(r * big, (r + 1) * big)
        in_first = lax.broadcasted_iota(jnp.int32, (big, 1), 0) + r * big < first
        a = dot(waves_t[rows, :], prod[:, :channels])
        b = dot(waves_t[rows, :], prod[:, channels:])
        total = jnp.where(in_first, a, b) + skip[row, :] * mgrad[rows, :]
        one, two = ds[rows, mid], ds[rows, end]
        ds[rows, mid] = total * two
        ds[rows, end] = total * one
    for stream in range(STREAMS):
        cols = slice(stream * channels, (stream + 1) * channels)
        at = stream * SHORT
        bias_sum = jnp.zeros((1, channels), f32)
        in_sum = jnp.zeros((1, channels), f32)
        lag_sums = [jnp.zeros((1, channels), f32) for _ in range(SHORT)]
        for tile in range(tiles):
            rows = tile_rows(tile)
            _, offset = place(tile, first)
            d = ds[rows, cols]
            p = proj[rows, cols]
            total = d * conv_w[stream, 0, row, :]
            bias_sum = bias_sum + jnp.sum(d, axis=0, keepdims=True)
            lag_sums[0] = lag_sums[0] + jnp.sum(d * p, axis=0, keepdims=True)
            for lag in range(1, SHORT):
                _, later = place(tile, first, lag)
                moved = jnp.where(later >= lag, ahead(ds, tile, cols, lag, tiles - 1), 0.0)
                total = total + moved * conv_w[stream, lag, row, :]
                lag_sums[lag] = lag_sums[lag] + jnp.sum(moved * p, axis=0, keepdims=True)
            in_sum = in_sum + jnp.sum(total, axis=0, keepdims=True)
            in_low[rows, cols] = total.astype(bf16)
        sums[ROW_IN_BIAS + stream : ROW_IN_BIAS + stream + 1, :] = in_sum
        sums[ROW_CONV_B + stream : ROW_CONV_B + stream + 1, :] = bias_sum
        for lag in range(SHORT):
            sums[ROW_CONV_W + at + lag : ROW_CONV_W + at + lag + 1, :] = lag_sums[lag]

    def into(at):
        rows = pl.ds(at, block)
        total = dot_cols(in_low[rows, :channels], in_w[0])
        for stream in range(1, STREAMS):
            cols = slice(stream * channels, (stream + 1) * channels)
            total = total + dot_cols(in_low[rows, cols], in_w[stream])
        return total

    copies[8].wait()
    for half, (sent, keep) in enumerate(((sent_a, keep_a), (sent_b, keep_b))):
        at = pl.multiple_of(2 * block * half + (1 - core) * block, block)
        sent[...] = into(at).astype(bf16)
        at = pl.multiple_of(2 * block * half + core * block, block)
        keep[...] = into(at)
    taps_grad[...] = dot(waves_t[:REACH, :], corr[...]) * (2.0 / WAVES)


def mix_bwd(run, layer, scal, rows, out_w, saved, spec, in_w, conv_w, conv_b, skip, taps, waves, waves_t):
    block, channels = rows[0].shape[0], skip.shape[1]
    length = 4 * block
    return run(
        functools.partial(mix_bwd_kernel, layer),
        [(scal, SMALL)]
        + [(a, None) for a in (conv_w, conv_b, skip)]
        + [(stay(a), FAR) for a in rows[:2]]
        + [(a, FAR) for a in rows[2:]]
        + [(stay(out_w), FAR)]
        + [(stay(a), FAR) for a in (saved[0][0], saved[1][0], saved[0][1], saved[1][1], waves, spec, taps, waves_t, in_w)],
        [
            struct((length, STREAMS * channels), bf16),
            struct((REACH, channels), f32),
            struct((16, channels), f32),
            struct((block, D), bf16),
            struct((block, D), bf16),
            struct((block, D), f32),
            struct((block, D), f32),
        ],
        scratch=[
            pltpu.VMEM((block, D), bf16),
            pltpu.VMEM((block, D), bf16),
            pltpu.VMEM((block, D), bf16),
            pltpu.VMEM((block, D), bf16),
            pltpu.VMEM((channels, D), bf16),
            pltpu.VMEM((length, STREAMS * channels), f32),
            pltpu.VMEM((length, channels), f32),
            pltpu.VMEM((WAVES, length), bf16),
            pltpu.VMEM((WAVES, 2 * channels), bf16),
            pltpu.VMEM((WAVES, channels), f32),
            pltpu.VMEM((length, WAVES), bf16),
            pltpu.VMEM((STREAMS, D, channels), bf16),
            pltpu.VMEM((length, channels), f32),
            pltpu.VMEM((length, STREAMS * channels), f32),
            pltpu.VMEM((length, 2 * channels), bf16),
            pltpu.VMEM((WAVES, 2 * channels), bf16),
            pltpu.VMEM((WAVES, channels), bf16),
            pltpu.SemaphoreType.DMA((14,)),
        ],
        name="mix_bwd",
    )


def parts_order(strides):
    bits = len(strides)
    return [sum(((part >> (bits - 1 - i)) & 1) * s for i, s in enumerate(strides)) for part in range(1 << bits)]


def spread_columns(source, target, at, index, order):
    for part, step in enumerate(order):
        cols = pl.ds(pl.multiple_of((index ^ step) * CHUNK, CHUNK), CHUNK)
        target[at, part * CHUNK : (part + 1) * CHUNK] = source[:, cols]


def ffn_grad_kernel(orders, scal, *refs):
    feeds, lows = refs[0:4], refs[4:8]
    (up_a, up_b, hid_a, hid_b), outs, (left, right) = refs[8:12], refs[12:16], refs[16:18]
    block = feeds[0].shape[0]
    index = scal[3]
    for k, (source, (rhs_a, rhs_b)) in enumerate(((feeds, (up_a, up_b)), (lows, (hid_a, hid_b)))):
        right[: 2 * block, :] = rhs_a[...]
        right[2 * block :, :] = rhs_b[...]
        for i in range(4):
            spread_columns(source[i], left, slice(i * block, (i + 1) * block), index, orders[k])
        for half in range(2):
            out = outs[2 * k + half]
            wide = PARTS // 2 * CHUNK
            got = dot_rows(left[:, half * wide : (half + 1) * wide], right[...]).astype(bf16)
            for part in range(PARTS // 2):
                out[part] = got[part * CHUNK : (part + 1) * CHUNK, :]


def ffn_whole_kernel(*refs):
    feeds, lows = refs[0:4], refs[4:8]
    (up_a, up_b, hid_a, hid_b), out, (left, right) = refs[8:12], refs[12], refs[13:15]
    block = feeds[0].shape[0]
    for k, (source, (rhs_a, rhs_b)) in enumerate(((feeds, (up_a, up_b)), (lows, (hid_a, hid_b)))):
        right[: 2 * block, :] = rhs_a[...]
        right[2 * block :, :] = rhs_b[...]
        for i in range(4):
            left[i * block : (i + 1) * block, :] = source[i][...]
        for half in range(2):
            rows = slice(half * D // 2, (half + 1) * D // 2)
            out[k, rows, :] = dot_rows(left[:, rows], right[...]).astype(bf16)


def ffn_whole(run, feeds, lows, ups, hids):
    block, width = feeds[0].shape[0], ups[0].shape[1]
    return run(
        ffn_whole_kernel,
        [(a, None) for a in (*feeds, *lows, *ups, *hids)],
        [struct((2, D, width), bf16)],
        scratch=[pltpu.VMEM((4 * block, D), bf16), pltpu.VMEM((4 * block, width), bf16)],
        spill=1,
        name="ffn_whole",
    )[0]


def ffn_grad(run, orders, scal, feeds, lows, ups, hids):
    block, width = feeds[0].shape[0], ups[0].shape[1]
    out = struct((PARTS // 2, CHUNK, width), bf16)
    return run(
        functools.partial(ffn_grad_kernel, orders),
        [(scal, SMALL)] + [(a, None) for a in (*feeds, *lows, *ups, *hids)],
        [out] * 4,
        scratch=[pltpu.VMEM((4 * block, D), bf16), pltpu.VMEM((4 * block, width), bf16)],
        spill=4,
        name="ffn_grad",
    )


def join(target, a, b):
    rows = a.shape[0]
    target[:rows, :] = a[...]
    target[rows:, :] = b[...]


def mix_grad_kernel(orders, scal, *refs):
    normed, lows = refs[0:4], refs[4:8]
    in_low, mixed_a, mixed_b = refs[8:11]
    outs, (left, mixed) = refs[11:-2], refs[-2:]
    joined = len(outs) == 2
    channels = mixed.shape[1]
    join(mixed, mixed_a, mixed_b)
    core, index = scal[1], scal[3]
    groups = (
        (normed, in_low, slice(0, 2 * channels), 0, 0),
        (normed, in_low, slice(2 * channels, 3 * channels), 1, 0),
        (lows, mixed, slice(0, channels), 1, 1),
    )
    for source, rhs, cols, group, base in groups:
        own_a, own_b, got_a, got_b = source
        block = own_a.shape[0]
        for rows, at in halves(own_a, own_b, got_a, got_b, core):
            spread_columns(rows, left, pl.ds(at, block), index, orders[group])
        for half in range(2):
            out = outs[half if joined else 2 * group + half]
            first = base + 2 * group if joined else base
            wide = PARTS // 2 * CHUNK
            got = dot_rows(left[:, half * wide : (half + 1) * wide], rhs[:, cols]).astype(bf16)
            for part in range(PARTS // 2):
                for i in range(got.shape[1] // channels):
                    block_cols = slice(i * channels, (i + 1) * channels)
                    out[part, first + i] = got[part * CHUNK : (part + 1) * CHUNK, block_cols]


def mix_grad(run, orders, scal, normed, lows, in_low, mixed, joined):
    block, channels = normed[0].shape[0], mixed[0].shape[1]
    if joined:
        outs = [struct((PARTS // 2, 4, CHUNK, channels), bf16)] * 2
    else:
        outs = [struct((PARTS // 2, 2, CHUNK, channels), bf16)] * 4
    return run(
        functools.partial(mix_grad_kernel, orders),
        [(scal, SMALL)]
        + [(a, None) for a in (*normed, *lows, in_low, *mixed)],
        outs,
        scratch=[pltpu.VMEM((4 * block, D), bf16), pltpu.VMEM((4 * block, channels), bf16)],
        spill=len(outs),
        name="mix_grad",
    )


def halve_kernel(keep, got, sent, kept):
    count = keep.shape[0] // 2
    for i in range(count):
        kept[i] = (keep[i].astype(f32) + got[i].astype(f32)).astype(bf16)
        sent[i] = (keep[count + i].astype(f32) + got[count + i].astype(f32)).astype(bf16)


def halve(run, keep, got):
    out = struct((keep.shape[0] // 2, *keep.shape[1:]), bf16)
    return run(halve_kernel, [(keep, None), (got, None)], [out, out], spill=2, name="halve")


def total_of(refs, leads):
    return sum(ref[lead].astype(f32) for ref, lead in zip(refs, leads))


def finish_kernel(leads, turned, *refs):
    out, refs = refs[-1], list(refs[:-1])
    for layer, lead in enumerate(leads):
        total = total_of([refs.pop(0) for _ in lead], lead)
        out[layer] = total.T if turned else total


def ffn_finish(run, terms, turned):
    _, rows, cols = terms[0][0][0].shape
    shape = (cols, rows) if turned else (rows, cols)
    leads = [[lead for _, lead in pairs] for pairs in terms]
    return run(
        functools.partial(finish_kernel, leads, turned),
        [(a, None) for pairs in terms for a, _ in pairs],
        [struct((len(terms), *shape), f32)],
        name="ffn_finish",
    )[0]


def mix_finish_kernel(plan, *refs):
    into, out = refs[-2:]
    for layer, streams in enumerate(plan):
        for stream, parts in enumerate(streams):
            total = sum(refs[k][lead].astype(f32) for k, lead in parts)
            if stream < STREAMS:
                into[layer, stream] = total
            else:
                out[layer] = total.T


def mix_finish(run, arrays, plan):
    rows, channels = arrays[0].shape[-2:]
    return run(
        functools.partial(mix_finish_kernel, plan),
        [(a, None) for a in arrays],
        [struct((len(plan), STREAMS, rows, channels), f32), struct((len(plan), channels, rows), f32)],
        name="mix_finish",
    )


def pack_kernel(mix, filt, narrow, up_a, up_b, feed_a, feed_b, in_a, in_b, own, down, out):
    channels = mix.shape[1]
    out[:16, :] = mix[...]
    out[ROW_FILTER : ROW_FILTER + FILT, :] = filt[...]
    for q in range(D // channels):
        cols = slice(q * channels, (q + 1) * channels)
        out[ROW_UP_BIAS + q : ROW_UP_BIAS + q + 1, :] = up_a[:, cols] + up_b[:, cols]
        wide = [feed_a[i : i + 1, cols] + feed_b[i : i + 1, cols] for i in range(3)]
        wide.append(down[:, cols])
        wide += [in_a[i : i + 1, cols] + in_b[i : i + 1, cols] for i in range(2)]
        wide += [own[i : i + 1, cols] for i in range(2)]
        for i, value in enumerate(wide):
            at = ROW_WIDE + 4 * i + q
            out[at : at + 1, :] = value
    groups = [
        narrow[i * NARROW_GROUP : (i + 1) * NARROW_GROUP, :] for i in range(channels // FILT)
    ]
    out[ROW_NARROW:, :] = jnp.concatenate(groups, axis=1)


def pack(run, mix, filt, narrow, ups, feeds, ins, own, down):
    return run(
        pack_kernel,
        [(a, None) for a in (mix, filt, narrow, *ups, *feeds, *ins, own, down)],
        [struct((PACK_ROWS, mix.shape[1]), f32)],
        name="pack_small",
    )[0]


def gate(run, after=()):
    run(lambda: None, [], [], name="gate", after=after)


def stack_kernel(*refs):
    size = refs[0].shape[0]
    total, low = refs[-2:]
    for i, ref in enumerate(refs[:-2]):
        total[i * size : (i + 1) * size, :] = ref[...]
        low[i * size : (i + 1) * size, :] = ref[...].astype(bf16)


def stack_packs(run, packs):
    rows, cols = packs[0].shape
    shape = (len(packs) * rows, cols)
    return run(
        stack_kernel, [(a, None) for a in packs], [struct(shape, f32), struct(shape, bf16)], name="stack_packs"
    )


def add_small_kernel(value, got, total, low):
    added = value[...] + got[...].astype(f32)
    total[...] = added
    low[...] = added.astype(bf16)


def add_small(run, value, got):
    outs = [struct(value.shape, f32), struct(value.shape, bf16)]
    return run(add_small_kernel, [(value, None), (got, None)], outs, name="add_small")


def last_small_kernel(value, got, total, wide):
    added = value[...] + got[...].astype(f32)
    total[...] = added
    size = PACK_ROWS - ROW_WIDE
    for i in range(value.shape[0] // PACK_ROWS):
        wide[i * size : (i + 1) * size, :] = added[i * PACK_ROWS + ROW_WIDE : (i + 1) * PACK_ROWS, :]


def last_small(run, value, got):
    rows, cols = value.shape
    wide = struct((rows // PACK_ROWS * (PACK_ROWS - ROW_WIDE), cols), f32)
    return run(
        last_small_kernel, [(value, None), (got, None)], [struct(value.shape, f32), wide], name="last_small"
    )


def sum_kernel(a, b, out):
    out[...] = a[...] + b[...]


def add_pair(run, a, b):
    return run(sum_kernel, [(a, None), (b, None)], [struct(a.shape, f32)], name="add_pair")[0]


def unpack_kernel(layers, *refs):
    (chans, wides), outs = refs[:2], refs[2:]
    (gain, shift, out_bias, feed_gain, feed_shift, down_bias, in_bias, conv_w, conv_b, skip, filt, up_bias,
     w_in, b_in, f_in, w_mid, b_mid, f_mid) = outs
    channels = chans.shape[1]
    size = PACK_ROWS - ROW_WIDE
    for layer in range(layers):
        chan = chans[layer * PACK_ROWS : (layer + 1) * PACK_ROWS, :]
        wide = wides[layer * size : (layer + 1) * size, :]
        row = slice(layer, layer + 1)

        def spread(target, ref, at, row=row):
            for q in range(D // channels):
                target[row, q * channels : (q + 1) * channels] = ref[at + q : at + q + 1, :]

        spread(feed_gain, wide, 0)
        spread(feed_shift, wide, 4)
        spread(out_bias, wide, 8)
        spread(down_bias, wide, 12)
        if layer + 1 < layers:
            spread(gain, wide, 16, slice(layer + 1, layer + 2))
            spread(shift, wide, 20, slice(layer + 1, layer + 2))
        if layer == 0:
            spread(gain, wide, 24)
            spread(shift, wide, 28)
        spread(up_bias, chan, ROW_UP_BIAS)
        for stream in range(STREAMS):
            in_bias[stream, row, :] = chan[ROW_IN_BIAS + stream : ROW_IN_BIAS + stream + 1, :]
            conv_b[stream, row, :] = chan[ROW_CONV_B + stream : ROW_CONV_B + stream + 1, :]
            for lag in range(SHORT):
                at = ROW_CONV_W + stream * SHORT + lag
                conv_w[stream, lag, row, :] = chan[at : at + 1, :]
        skip[row, :] = chan[ROW_SKIP : ROW_SKIP + 1, :]
        filt[layer] = chan[ROW_FILTER : ROW_FILTER + FILT, :]
        base = ROW_NARROW - ROW_WIDE
        rows = slice(base, base + NARROW_GROUP)
        narrow = jnp.concatenate(
            [wide[rows, i * FILT : (i + 1) * FILT] for i in range(channels // FILT)], axis=0
        )
        for target, at in ((b_in, NB_IN), (f_in, NF_IN), (b_mid, NB_MID), (f_mid, NF_MID)):
            target[row, :] = narrow[at : at + 1, :]
        w_in[layer] = narrow[:POS, :]
        w_mid[layer] = narrow[NW_MID : NW_MID + FILT, :]


def unpack(run, chans, wides, up_width):
    layers, channels = chans.shape[0] // PACK_ROWS, chans.shape[1]
    return run(
        functools.partial(unpack_kernel, layers),
        [(chans, None), (wides, None)],
        [struct((layers, D), f32)] * 6
        + [
            struct((STREAMS, layers, channels), f32),
            struct((STREAMS, SHORT, layers, channels), f32),
            struct((STREAMS, layers, channels), f32),
            struct((layers, channels), f32),
            struct((layers, FILT, channels), f32),
            struct((layers, up_width), f32),
            struct((layers, POS, FILT), f32),
            struct((layers, FILT), f32),
            struct((layers, FILT), f32),
            struct((layers, FILT, FILT), f32),
            struct((layers, FILT), f32),
            struct((layers, FILT), f32),
        ],
        name="unpack_small",
    )


def dp_swap(x, stride):
    size = lax.axis_size("dp")
    return lax.ppermute(x, "dp", [(i, i ^ stride) for i in range(size)])


class Scatter:
    def __init__(self, run, sent, keep, strides):
        self.run, self.keep = run, keep
        self.strides = list(strides)
        self.got = dp_swap(sent, self.strides.pop(0))

    def step(self):
        sent, self.keep = halve(self.run, self.keep, self.got)
        self.got = dp_swap(sent, self.strides.pop(0))

    def pair(self):
        while self.strides:
            self.step()
        return self.keep, self.got


class SmallSum:
    def __init__(self, run, packs, strides):
        self.run, self.strides = run, list(strides)
        self.value, low = stack_packs(run, packs)
        self.got = dp_swap(low, self.strides.pop(0))

    def step(self):
        self.value, low = add_small(self.run, self.value, self.got)
        self.got = dp_swap(low, self.strides.pop(0))

    def sums(self):
        return last_small(self.run, self.value, self.got)


def share_out(pair):
    keep, got = pair
    total = (keep[0].astype(f32) + got[0].astype(f32)).reshape(-1, CHUNK, keep.shape[-1])
    left = lax.axis_size("dp") // PARTS
    index = lax.axis_index("dp")
    stride = 1
    total = total.reshape(total.shape[0], left, CHUNK // left, -1)
    while left > 1:
        total = total.reshape(total.shape[0], left // 2, 2, total.shape[2], -1)
        bit = (index // stride) % 2
        mine = lax.dynamic_index_in_dim(total, bit, 2, keepdims=False)
        other = lax.dynamic_index_in_dim(total, 1 - bit, 2, keepdims=False)
        total = mine + dp_swap(other.astype(bf16), stride).astype(f32)
        left, stride = left // 2, stride * 2
    return total[:, 0]


def shards(
    tokens,
    seg_lengths,
    cotangent,
    mixer_norm_gain,
    mixer_norm_bias,
    in_weight,
    in_bias,
    conv_weight,
    conv_bias,
    filter_in,
    filter_in_bias,
    filter_in_freq,
    filter_mid,
    filter_mid_bias,
    filter_mid_freq,
    filter_out,
    skip_bias,
    out_weight,
    out_bias,
    feed_norm_gain,
    feed_norm_bias,
    feed_up,
    feed_up_bias,
    feed_down,
    feed_down_bias,
):
    block = tokens.shape[1]
    length = block * lax.axis_size("mp")
    channels = in_weight.shape[3]
    layers = in_weight.shape[0]
    spot = lax.axis_index("mp").astype(jnp.int32)
    left = lax.axis_size("dp") // PARTS
    chunk = (lax.axis_index("dp") // left).astype(jnp.int32)
    scal = jnp.stack([seg_lengths[0, 0], spot % 2, spot // 2, chunk, spot])
    table = wave_table(length)
    waves = jnp.asarray(table)
    waves_t = jnp.asarray(np.ascontiguousarray(table.T))
    pos = jnp.asarray(position_table(length))
    run = Chain()

    in_w = in_weight.transpose(0, 2, 1, 3)
    in_b = in_bias.transpose(1, 0, 2)
    conv_w = conv_weight.transpose(1, 2, 0, 3)
    conv_b = conv_bias.transpose(1, 0, 2)
    filter_weights = (
        filter_in, filter_in_bias, filter_in_freq, filter_mid, filter_mid_bias, filter_mid_freq, filter_out
    )
    both = range(2)

    def start_sum(ends):
        got = [core_swap(ends[i]) for i in both]
        out = []
        for i in both:
            here = add_low(run, ends[2 + i], got[i])
            out.append((here, chip_swap(here)))
        return out

    def one_sum(sent, keep):
        here = add_low(run, keep, core_swap(sent))
        return here, chip_swap(here)

    def in_turn(first, pace=None):
        gate(run, [first[1]])
        if pace is None:
            gate(run)
        else:
            pace.step()

    mine = tokens[0]
    other = chip_swap(mine)
    filt = [None] * layers
    early = tuple(stay(a) for a in filter_weights)
    filt[0] = filter_fwd(run, 0, length, scal, stay(pos), early, stay(waves))
    low_a, low_b, res_a, res_b, cot = first_norm(
        run, scal, stay(mine), other, stay(mixer_norm_gain), stay(mixer_norm_bias), stay(cotangent[0])
    )
    res, low = [res_a, res_b], [low_a, low_b]

    def in_halves(prepare, work, sums):
        out = []
        for i in both:
            prepare(i)
            sent, keep = work(i)
            if i == 0 and sums is not None:
                in_turn(sums[1])
            if i == 1:
                in_turn(out[0])
            out.append(one_sum(sent, keep))
        return out

    stored, cot_parts = [], []
    back = [None, None]
    got = [core_swap(x) for x in low]
    cot_other = chip_swap(cot)
    sums = None
    for layer in range(layers):
        last = layer + 1 == layers
        saved, passed, middle, feed, feed_got, ffn = [], [None], [], [], [], []
        if layer:
            res, low, got = [], [], []

        def mix_prepare(i):
            if layer:
                b, a = add_norm(
                    run, layer - 1, layer, *sums[i], stored[layer - 1][5][i],
                    feed_down_bias, mixer_norm_gain, mixer_norm_bias, 1,
                )
                res.append(a)
                low.append(b)
                got.append(core_swap(b))

        def mix_work(i):
            kept, on, sent, keep = mix_fwd(
                run, layer, i, scal, low[i], got[i], in_w, in_b, conv_w, conv_b, skip_bias, filt[layer][0],
                out_weight, waves, waves_t, passed[-1],
            )
            saved.append(kept)
            passed.append(on)
            if layer == 0 and i == 0:
                cot_parts.extend(first_grad(run, scal, cot, cot_other))
            return sent, keep

        def feed_prepare(i):
            b, a = add_norm(run, layer, layer, *sums[i], res[i], out_bias, feed_norm_gain, feed_norm_bias)
            middle.append(a)
            feed.append(b)
            feed_got.append(core_swap(b))

        def feed_work(i):
            ffn.append(ffn_fwd(run, layer, feed[i], feed_got[i], feed_up, feed_up_bias, feed_down))
            if i == 0 and not last:
                filt[layer + 1] = filter_fwd(
                    run, layer + 1, length, scal, pos, filter_weights, waves
                )
            if not last:
                return ffn[i][2], ffn[i][3]
            back[i] = ffn_bwd(run, layer, cot_low[i], cot_got[i], feed_up, feed_down, ffn[i][0], True)
            return back[i][2], back[i][3]

        sums = in_halves(mix_prepare, mix_work, sums)
        if layer == 0:
            cot_sum, *cot_low = cot_parts
            cot_got = [core_swap(x) for x in cot_low]
        stored.append(
            (res, (*low, *got), saved, passed[2][1], [kept[2] for kept in saved], middle, feed, feed_got, ffn)
        )
        sums = in_halves(feed_prepare, feed_work, sums)
    back_sums = sums

    rising, turned = (1, 2, 4), (2, 4, 1)
    feed_orders, mix_orders = (rising, turned), (rising, rising)

    def scatter_pair(sends, orders):
        return [
            Scatter(run, sends[2 * k + 1], sends[2 * k], [left * o for o in orders[k]]) for k in range(2)
        ]

    def scatter_rows(whole_grad):
        return lax.psum_scatter(whole_grad, "dp", scatter_dimension=1, tiled=True)

    def grad_args(layer, low, got, back):
        feed, feed_got, ffn = stored[layer][6:]
        return (
            (feed[0], feed_got[0], feed[1], feed_got[1]),
            (low[0], got[0], low[1], got[1]),
            [back[i][1] for i in both],
            [ffn[i][1] for i in both],
        )

    grad, low, got = cot_low, cot_low, cot_got
    down_sum = cot_sum
    moves = back_sums
    feed_shares, mix_rest, packs = ([None] * layers for _ in range(3))
    no_sums = jnp.zeros((8, D), f32)
    in_sums = [no_sums, no_sums]
    for layer in reversed(range(layers)):
        above = layer + 1
        entry, normed, saved, spec, mixed, middle, feed, feed_got, ffn = stored[layer]
        if layer:
            feed_whole = ffn_whole(run, *grad_args(layer, low, got, back))
        else:
            feed_sends = ffn_grad(
                run, [parts_order(o) for o in feed_orders], scal, *grad_args(layer, low, got, back)
            )
        if above == layers:
            out_got = [core_swap(ffn[i][2]) for i in both]
            out_send, out_mine = pick_outputs(
                run, layer, scal, [ffn[i][3] for i in both], out_got, middle, feed_down_bias
            )
        new_grad, low, feed_sums = [], [], []
        for i in both:
            a, c, b = norm_back(run, layer, *moves[i], middle[i], grad[i], feed_norm_gain, 1)
            new_grad.append(a)
            low.append(b)
            feed_sums.append(c)
        grad = new_grad
        got = [core_swap(x) for x in low]
        rows = (*low, *got)
        if layer:
            feed_shares[layer] = scatter_rows(run.release([feed_whole])[0])
        else:
            feed_sends[1], feed_sends[3] = run.release([feed_sends[1], feed_sends[3]])
            up_big, down_big = scatter_pair(feed_sends, feed_orders)
        in_low, taps_grad, mix_sums, *ends = mix_bwd(
            run, layer, scal, rows, out_weight, saved, spec, in_w, conv_w, conv_b, skip_bias,
            filt[layer][0], waves, waves_t,
        )
        if layer:
            if above == layers:
                outputs = last_add(run, out_mine, chip_swap(out_send))
            moves = start_sum(ends)
            own_sums = no_sums
            mix_keep, mix_sent = mix_grad(
                run, [parts_order(rising)] * 2, scal, normed, rows, in_low, mixed, True
            )
        else:
            for x in mix_rest[1:]:
                x.step()
            swapped = [core_swap(ends[i]) for i in both]
        filt_out, narrow = filter_bwd(run, layer, length, scal, taps_grad, pos, filter_weights, filt[layer][1])
        if layer == 0:
            up_big.step()
            send, own, own_sums = last_pick(run, scal, ends[2:], swapped, entry)
            there = chip_swap(send)
            down_big.step()
        packs[layer] = pack(
            run, mix_sums, filt_out, narrow, [back[i][0] for i in both], feed_sums, in_sums, own_sums, down_sum
        )
        if layer == 0:
            small = SmallSum(
                run, packs, [1 << i for i in range(left.bit_length() - 1)] + [left * o for o in rising]
            )
            sends = mix_grad(
                run, [parts_order(o) for o in mix_orders], scal, normed, rows, in_low, mixed, False
            )
            small.step()
            sends[1], sends[3] = run.release([sends[1], sends[3]])
            mix_bigs = scatter_pair(sends, mix_orders)
            up_big.step()
            for x in mix_rest[1:]:
                x.step()
            break
        new_grad, new_low, in_sums, new_got, new_back, back_sums = [], [], [], [], [], []

        def norm_half(i):
            a, c, b = norm_back(run, layer, *moves[i], entry[i], grad[i], mixer_norm_gain)
            new_grad.append(a)
            new_low.append(b)
            in_sums.append(c)
            new_got.append(core_swap(b))

        def ffn_half(i):
            below = stored[layer - 1][8]
            new_back.append(
                ffn_bwd(run, layer - 1, new_low[i], new_got[i], feed_up, feed_down, below[i][0], False)
            )

        def sum_half(i):
            back_sums.append(one_sum(new_back[i][2], new_back[i][3]))

        norm_half(0)
        mix_rest[layer] = Scatter(run, run.release([mix_sent])[0], mix_keep, [left * o for o in rising])
        ffn_half(0)
        in_turn(moves[1])
        sum_half(0)
        norm_half(1)
        ffn_half(1)
        in_turn(back_sums[0])
        sum_half(1)
        moves = back_sums
        back = new_back
        down_sum = (in_sums[0] + in_sums[1])[2:3]
        grad, low, got = new_grad, new_low, new_got
    token_grad = last_back(run, 0, scal, own, there, entry, grad, mixer_norm_gain)
    while small.strides:
        small.step()
    down_big.step()
    mix_bigs[0].step()
    small_sums, wide = small.sums()
    wide_got = chip_swap(wide)
    mix_bigs[1].step()
    wide = add_pair(run, wide, wide_got)
    wide_got = core_swap(wide)
    mix_bigs[0].step()
    mix_bigs[1].step()
    (gain, shift, out_bias_g, feed_gain, feed_shift, down_bias_g, in_bias_g, conv_w_g, conv_b_g, skip_g, filt_g,
     up_bias_g, w_in_g, b_in_g, f_in_g, w_mid_g, b_mid_g, f_mid_g) = unpack(
        run, small_sums, add_pair(run, wide, wide_got), feed_up.shape[2]
    )
    up_pair, down_pair = up_big.pair(), down_big.pair()
    if left == 1:
        up_first, down_first = [[(a, 0) for a in pair] for pair in (up_pair, down_pair)]
    else:
        up_first, down_first = [[(share_out(pair), 0)] for pair in (up_pair, down_pair)]
    up_g = ffn_finish(run, [up_first] + [[(a, 0)] for a in feed_shares[1:]], False)
    down_g = ffn_finish(run, [down_first] + [[(a, 1)] for a in feed_shares[1:]], True)
    mix_pairs = [x.pair() for x in mix_bigs]
    if left == 1:
        arrays = [a for pair in mix_pairs for a in pair]
        first = [[(2 * k, (0, i)), (2 * k + 1, (0, i))] for k in both for i in both]
    else:
        arrays = [share_out(pair) for pair in mix_pairs]
        first = [[(k, i)] for k in both for i in both]
    plan = [first]
    for x in mix_rest[1:]:
        pair = x.pair()
        if left == 1:
            plan.append([[(len(arrays), (0, i)), (len(arrays) + 1, (0, i))] for i in range(STREAMS + 1)])
            arrays += pair
        else:
            plan.append([[(len(arrays), i)] for i in range(STREAMS + 1)])
            arrays.append(share_out(pair))
    in_g, out_g = mix_finish(run, arrays, plan)
    return (
        outputs[None],
        token_grad[None],
        gain,
        shift,
        in_g.transpose(0, 2, 1, 3),
        in_bias_g.transpose(1, 0, 2),
        conv_w_g.transpose(2, 0, 1, 3),
        conv_b_g.transpose(1, 0, 2),
        w_in_g,
        b_in_g,
        f_in_g,
        w_mid_g,
        b_mid_g,
        f_mid_g,
        filt_g,
        skip_g,
        out_g,
        out_bias_g,
        feed_gain,
        feed_shift,
        up_g,
        up_bias_g,
        down_g,
        down_bias_g,
    )


def solution(mesh):
    in_specs = (
        P("dp", "mp", None),
        P("dp", None),
        P("dp", "mp", None),
        P(),
        P(),
        P(None, None, None, "mp"),
        P(None, None, "mp"),
        P(None, None, None, "mp"),
        P(None, None, "mp"),
        P(),
        P(),
        P(),
        P(),
        P(),
        P(),
        P(None, None, "mp"),
        P(None, "mp"),
        P(None, "mp", None),
        P(),
        P(),
        P(),
        P(None, None, "mp"),
        P(None, "mp"),
        P(None, "mp", None),
        P(),
    )
    out_specs = (
        P("dp", "mp", None),
        P("dp", "mp", None),
        P(),
        P(),
        P(None, "dp", None, "mp"),
        P(None, None, "mp"),
        P(None, None, None, "mp"),
        P(None, None, "mp"),
        P(),
        P(),
        P(),
        P(),
        P(),
        P(),
        P(None, None, "mp"),
        P(None, "mp"),
        P(None, "mp", "dp"),
        P(),
        P(),
        P(),
        P(None, "dp", "mp"),
        P(None, "mp"),
        P(None, "mp", "dp"),
        P(),
    )
    return jax.shard_map(shards, mesh=mesh, in_specs=in_specs, out_specs=out_specs, check_vma=False)
```

profile of v0, /device:TPU:0, one launch (start us, length us, event | category | flops | bytes accessed | tf_op | source)
XLA Modules:
  0.0 373.1 jit_solution(9125251176667781980)
XLA Ops:
  12.4 8.2 %filter_fwd.2 = (f32[1792,256]{1,0:T(8,128)}, f32[6,64,896]{2,1,0:T(8,128)}, f32[8,128]{1,0:T(8,128)}) custom-call(s32[5]{0:T(128)S(1)} %stack.19.refs_0_, f32[64,896]{1,0:T(8,128)} %constant.52.clone.refs_1_.refs_2_, f32[2,33,64]{2,1,0:T(8,128)} %copy.58.refs_2_, f32[2,64]{1,0:T(2,128)} %refs_3_.25, f32[2,64]{1,0:T(2,128)} %refs_3_.41, ...), custom_call_target="tpu_custom_call" | custom-call | flops 1 | bytes 1 | tf_op jit(solution)/shard_map/filter_fwd/pallas_call | solution.py:161
  27.6 7.6 %mix_fwd.4 = (f32[512,768]{1,0:T(8,128)}, f32[512,256]{1,0:T(8,128)}, bf16[512,256]{1,0:T(8,128)(2,1)}, bf16[1792,512]{1,0:T(8,128)(2,1)S(1)}, f32[8,768]{1,0:T(...) custom-call(s32[5]{0:T(128)S(1)} %stack.19.refs_0_, ...), custom_call_target="tpu_custom_call" | custom-call | flops 1 | bytes 1 | tf_op jit(solution)/shard_map/mix_fwd/pallas_call | solution.py:161
  35.8 4.0 %collective-permute-done.3.refs_2_ = bf16[256,1024]{1,0:T(8,128)(2,1)S(1)} collective-permute-done((bf16[256,1024]{1,0:T(8,128)(2,1)S(1)}, bf16[256,1024]{1,0:T(8,128)(2,1)S(1)}, u32[]{:S(2)}, u32[]{:S(2)}) %collective-permute-start.3) | collective-permute-done | bytes 524320 | tf_op jit(solution)/shard_map/ppermute | solution.py:74
  43.0 9.8 %mix_fwd.5 = (f32[512,768]{1,0:T(8,128)}, f32[512,256]{1,0:T(8,128)}, bf16[512,256]{1,0:T(8,128)(2,1)}, bf16[1792,512]{1,0:T(8,128)(2,1)}, f32[8,768]{1,0:T(8,12...) custom-call(s32[5]{0:T(128)S(1)} %stack.19.refs_0_, f32[3,2,256]{2,1,0:T(2,128)S(1)} %bitcast.31, ...), custom_call_target="tpu_custom_call" | custom-call | flops 1 | bytes 1 | tf_op jit(solution)/shard_map/mix_fwd/pallas_call | solution.py:161
  61.9 6.5 %filter_fwd.3 = (f32[1792,256]{1,0:T(8,128)}, f32[6,64,896]{2,1,0:T(8,128)}, f32[8,128]{1,0:T(8,128)}) custom-call(s32[5]{0:T(128)S(1)} %stack.19.refs_0_, f32[64,896]{1,0:T(8,128)S(1)} %copy-done.9, f32[2,33,64]{2,1,0:T(8,128)S(1)} %copy-done.72, f32[2,64]{1,0:T(2,128)S(1)} %copy-done.114, f32[2,64]{1,0:T(2,128)S(1)} %copy-done.103, ...), custom_call_target="tpu_custom_call" | custom-call | flops 1 | bytes 1 | tf_op jit(solution)/shard_map/filter_fwd/pallas_call | solution.py:161
  76.3 8.8 %collective-permute-done.10.refs_1_ = bf16[256,1024]{1,0:T(8,128)(2,1)S(1)} collective-permute-done((bf16[256,1024]{1,0:T(8,128)(2,1)S(1)}, bf16[256,1024]{1,0:T(8,128)(2,1)S(1)}, u32[]{:S(2)}, u32[]{:S(2)}) %collective-permute-start.10) | collective-permute-done | bytes 524320 | tf_op jit(solution)/shard_map/ppermute | solution.py:74
  88.8 7.5 %mix_fwd.6 = (f32[512,768]{1,0:T(8,128)}, f32[512,256]{1,0:T(8,128)}, bf16[512,256]{1,0:T(8,128)(2,1)}, bf16[1792,512]{1,0:T(8,128)(2,1)S(1)}, f32[8,768]{1,0:T(...) custom-call(s32[5]{0:T(128)S(1)} %stack.19.refs_0_, ...), custom_call_target="tpu_custom_call" | custom-call | flops 1 | bytes 1 | tf_op jit(solution)/shard_map/mix_fwd/pallas_call | solution.py:161
  96.5 4.5 %collective-permute-done.15.refs_1_ = bf16[256,1024]{1,0:T(8,128)(2,1)S(1)} collective-permute-done((bf16[256,1024]{1,0:T(8,128)(2,1)S(1)}, bf16[256,1024]{1,0:T(8,128)(2,1)S(1)}, u32[]{:S(2)}, u32[]{:S(2)}) %collective-permute-start.15) | collective-permute-done | bytes 524320 | tf_op jit(solution)/shard_map/ppermute | solution.py:74
  104.7 9.3 %mix_fwd.7 = (f32[512,768]{1,0:T(8,128)}, f32[512,256]{1,0:T(8,128)}, bf16[512,256]{1,0:T(8,128)(2,1)}, bf16[1792,512]{1,0:T(8,128)(2,1)}, f32[8,768]{1,0:T(8,12...) custom-call(s32[5]{0:T(128)S(1)} %stack.19.refs_0_, f32[3,2,256]{2,1,0:T(2,128)S(1)} %bitcast.33, ...), custom_call_target="tpu_custom_call" | custom-call | flops 1 | bytes 1 | tf_op jit(solution)/shard_map/mix_fwd/pallas_call | solution.py:161
  123.2 5.7 %ffn_bwd.4 = (bf16[512,1024]{1,0:T(8,128)(2,1)}, f32[1,1024]{1,0:T(1,128)}, bf16[256,1024]{1,0:T(8,128)(2,1)S(1)}, f32[256,1024]{1,0:T(8,128)S(1)}, f32[8,128]{1,0:T(8,128)}) custom-call(bf16[256,1024]{1,0:T(8,128)(2,1)S(1)} %get-tuple-element.370.refs_0_.refs_4_.refs_3_, bf16[256,1024]{1,0:T(8,128)(2,1)S(1)} %collective-permute-done.22.refs_1_.refs_5_, ...), custom_call_target="tpu_custom_call" | custom-call | flops 1 | bytes 1 | tf_op jit(solution)/shard_map/ffn_bwd/pallas_call | solution.py:161
  138.3 5.7 %ffn_bwd.5 = (bf16[512,1024]{1,0:T(8,128)(2,1)}, f32[1,1024]{1,0:T(1,128)}, bf16[256,1024]{1,0:T(8,128)(2,1)S(1)}, f32[256,1024]{1,0:T(8,128)S(1)}, f32[8,128]{1,0:T(8,128)}) custom-call(bf16[256,1024]{1,0:T(8,128)(2,1)S(1)} %get-tuple-element.383.refs_0_.refs_6_.refs_3_, bf16[256,1024]{1,0:T(8,128)(2,1)S(1)} %collective-permute-done.26.refs_1_.refs_7_, ...), custom_call_target="tpu_custom_call" | custom-call | flops 1 | bytes 1 | tf_op jit(solution)/shard_map/ffn_bwd/pallas_call | solution.py:161
  150.2 6.5 %ffn_whole.1 = (bf16[2,1024,1024]{2,1,0:T(8,128)(2,1)}, f32[8,128]{1,0:T(8,128)}) custom-call(bf16[256,1024]{1,0:T(8,128)(2,1)S(1)} %get-tuple-element.364.refs_0_, bf16[256,1024]{1,0:T(8,128)(2,1)S(1)} %collective-permute-done.19.refs_1_, bf16[256,1024]{1,0:T(8,128)(2,1)S(1)} %get-tuple-element.377.refs_0_.refs_2_, ...), custom_call_target="tpu_custom_call" | custom-call | flops 1 | bytes 1 | tf_op jit(solution)/shard_map/ffn_whole/pallas_call | solution.py:161
  166.2 16.3 %mix_bwd.2 = (bf16[1024,768]{1,0:T(8,128)(2,1)S(1)}, f32[896,256]{1,0:T(8,128)S(1)}, f32[16,256]{1,0:T(8,128)S(1)}, bf16[256,1024]{1,0:T(8,128)(2,1)S(1)}, bf16[...) custom-call(s32[5]{0:T(128)S(1)} %stack.19.refs_0_, ...), custom_call_target="tpu_custom_call" | custom-call | flops 1 | bytes 1 | tf_op jit(solution)/shard_map/mix_bwd/pallas_call | solution.py:161
  187.5 5.8 %mix_grad.2 = (bf16[4,4,128,256]{3,2,1,0:T(8,128)(2,1)}, bf16[4,4,128,256]{3,2,1,0:T(8,128)(2,1)}, f32[8,128]{1,0:T(8,128)}) custom-call(s32[5]{0:T(128)S(1)} %stack.19.refs_0_, bf16[256,1024]{1,0:T(8,128)(2,1)S(1)} %copy-done.17, bf16[256,1024]{1,0:T(8,128)(2,1)S(1)} %copy-done.20, bf16[256,1024]{1,0:T(8,128)(2,1)S(1)} %copy-done.19, ...), custom_call_target="tpu_custom_call" | custom-call | flops 1 | bytes 1 | tf_op jit(solution)/shard_map/mix_grad/pallas_call | solution.py:161
  203.8 7.4 %ffn_bwd.6 = (bf16[512,1024]{1,0:T(8,128)(2,1)}, f32[1,1024]{1,0:T(1,128)}, bf16[256,1024]{1,0:T(8,128)(2,1)S(1)}, f32[256,1024]{1,0:T(8,128)S(1)}, f32[8,128]{1,0:T(8,128)}) custom-call(bf16[256,1024]{1,0:T(8,128)(2,1)} %get-tuple-element.438.refs_0_.refs_5_, bf16[256,1024]{1,0:T(8,128)(2,1)} %collective-permute-done.36.refs_1_.refs_6_, ...), custom_call_target="tpu_custom_call" | custom-call | flops 1 | bytes 1 | tf_op jit(solution)/shard_map/ffn_bwd/pallas_call | solution.py:161
  211.4 4.8 %collective-permute-done.38.refs_1_ = bf16[256,1024]{1,0:T(8,128)(2,1)} collective-permute-done((bf16[256,1024]{1,0:T(8,128)(2,1)}, bf16[256,1024]{1,0:T(8,128)(2,1)}, u32[]{:S(2)}, u32[]{:S(2)}) %collective-permute-start.38) | collective-permute-done | bytes 524320 | tf_op jit(solution)/shard_map/ppermute | solution.py:74
  221.4 6.7 %ffn_bwd.7 = (bf16[512,1024]{1,0:T(8,128)(2,1)}, f32[1,1024]{1,0:T(1,128)}, bf16[256,1024]{1,0:T(8,128)(2,1)S(1)}, f32[256,1024]{1,0:T(8,128)S(1)}, f32[8,128]{1,0:T(8,128)}) custom-call(bf16[256,1024]{1,0:T(8,128)(2,1)S(1)} %get-tuple-element.451.refs_0_.refs_7_, bf16[256,1024]{1,0:T(8,128)(2,1)S(1)} %collective-permute-done.40.refs_1_.refs_8_, ...), custom_call_target="tpu_custom_call" | custom-call | flops 1 | bytes 1 | tf_op jit(solution)/shard_map/ffn_bwd/pallas_call | solution.py:161
  228.5 5.4 %collective-permute-done.39.refs_1_ = bf16[256,1024]{1,0:T(8,128)(2,1)S(1)} collective-permute-done((bf16[256,1024]{1,0:T(8,128)(2,1)S(1)}, bf16[256,1024]{1,0:T(8,128)(2,1)S(1)}, u32[]{:S(2)}, u32[]{:S(2)}) %collective-permute-start.39) | collective-permute-done | bytes 524320 | tf_op jit(solution)/shard_map/ppermute | solution.py:74
  238.3 7.7 %ffn_grad.1 = (bf16[4,128,1024]{2,1,0:T(8,128)(2,1)}, bf16[4,128,1024]{2,1,0:T(8,128)(2,1)}, bf16[4,128,1024]{2,1,0:T(8,128)(2,1)}, bf16[4,128,1024]{2,1,0:T(8,128)(2,1)}, f32[8,128]{1,0:T(8,128)}) custom-call(s32[5]{0:T(128)S(1)} %stack.19.refs_0_, bf16[256,1024]{1,0:T(8,128)(2,1)S(1)} %copy-done.32, bf16[256,1024]{1,0:T(8,128)(2,1)S(1)} %copy-done.34, ...), custom_call_target="tpu_custom_call" | custom-call | flops 1 | bytes 1 | tf_op jit(solution)/shard_map/ffn_grad/pallas_call | solution.py:161
  254.0 16.2 %mix_bwd.3 = (bf16[1024,768]{1,0:T(8,128)(2,1)S(1)}, f32[896,256]{1,0:T(8,128)S(1)}, f32[16,256]{1,0:T(8,128)S(1)}, bf16[256,1024]{1,0:T(8,128)(2,1)S(1)}, bf16[...) custom-call(s32[5]{0:T(128)S(1)} %stack.19.refs_0_, ...), custom_call_target="tpu_custom_call" | custom-call | flops 1 | bytes 1 | tf_op jit(solution)/shard_map/mix_bwd/pallas_call | solution.py:161
  277.9 6.7 %collective-permute-done.47.refs_1_ = bf16[4,128,1024]{2,1,0:T(8,128)(2,1)S(1)} collective-permute-done((bf16[4,128,1024]{2,1,0:T(8,128)(2,1)}, bf16[4,128,1024]{2,1,0:T(8,128)(2,1)S(1)}, u32[]{:S(2)}, u32[]{:S(2)}) %collective-permute-start.47) | collective-permute-done | bytes 1048608 | tf_op jit(solution)/shard_map/ppermute | solution.py:1296
  295.7 5.5 %mix_grad.3 = (bf16[4,2,128,256]{3,2,1,0:T(8,128)(2,1)}, bf16[4,2,128,256]{3,2,1,0:T(8,128)(2,1)}, bf16[4,2,128,256]{3,2,1,0:T(8,128)(2,1)}, bf16[4,2,128,256]{3,2,1,0:T(8,128)(2,1)}, f32[8,128]{1,0:T(8,128)}) custom-call(s32[5]{0:T(128)S(1)} %stack.19.refs_0_, bf16[256,1024]{1,0:T(8,128)(2,1)S(1)} %copy-done.10, bf16[256,1024]{1,0:T(8,128)(2,1)S(1)} %copy-done.12, ...), custom_call_target="tpu_custom_call" | custom-call | flops 1 | bytes 1 | tf_op jit(solution)/shard_map/mix_grad/pallas_call | solution.py:161
  334.9 4.0 %collective-permute-done.61.refs_1_ = bf16[2,2,128,256]{3,2,1,0:T(8,128)(2,1)S(1)} collective-permute-done((bf16[2,2,128,256]{3,2,1,0:T(8,128)(2,1)}, bf16[2,2,128,256]{3,2,1,0:T(8,128)(2,1)S(1)}, u32[]{:S(2)}, u32[]{:S(2)}) %collective-permute-start.61) | collective-permute-done | bytes 262176 | tf_op jit(solution)/shard_map/ppermute | solution.py:1296
  345.1 10.0 %collective-permute-done.67.refs_1_ = bf16[1,128,1024]{2,1,0:T(8,128)(2,1)S(1)} collective-permute-done((bf16[1,128,1024]{2,1,0:T(8,128)(2,1)S(1)}, bf16[1,128,1024]{2,1,0:T(8,128)(2,1)S(1)}, u32[]{:S(2)}, u32[]{:S(2)}) %collective-permute-start.67) | collective-permute-done | bytes 262176 | tf_op jit(solution)/shard_map/ppermute | solution.py:1296
  (458 shorter events, 176.0 us)
Async XLA Ops:
  7.2 347.9 %reduce-scatter.2.cloned.1.call-start = ((), (), s32[]{:S(2)}) async-start(), calls=%async_computation.1 | async-start | bytes 4718592 | tf_op jit(solution)/shard_map/reduce_scatter | solution.py:1505
  7.2 15.2 %collective-permute-start = (bf16[256,1024]{1,0:T(8,128)(2,1)}, bf16[256,1024]{1,0:T(8,128)(2,1)S(1)}, u32[]{:S(2)}, u32[]{:S(2)}) collective-permute-start(bf16[256,1024]{1,0:T(8,128)(2,1)} %bitcast.40), channel_id=1, source_target_pairs={{0,2},{1,3},{2,0},{3,1},{4,6},{5,7},{6,4},{7,5},{8,10},{9,11},{10,... | collective-permute-start | bytes 1572872 | tf_op jit(solution)/shard_map/ppermute | solution.py:74
  25.5 14.3 %collective-permute-start.3 = (bf16[256,1024]{1,0:T(8,128)(2,1)S(1)}, bf16[256,1024]{1,0:T(8,128)(2,1)S(1)}, u32[]{:S(2)}, u32[]{:S(2)}) collective-permute-start(bf16[256,1024]{1,0:T(8,128)(2,1)S(1)} %get-tuple-element.315.refs_1_), channel_id=1, source_target_pairs={{0,2},{1,3},{2,0},{3,1},{4,6},{5,7},{6,4},{7,5},{8,10},{9,11},{10,... | collective-permute-start | bytes 1572872 | tf_op jit(solution)/shard_map/ppermute | solution.py:74
  70.8 14.3 %collective-permute-start.10 = (bf16[256,1024]{1,0:T(8,128)(2,1)S(1)}, bf16[256,1024]{1,0:T(8,128)(2,1)S(1)}, u32[]{:S(2)}, u32[]{:S(2)}) collective-permute-start(bf16[256,1024]{1,0:T(8,128)(2,1)S(1)} %get-tuple-element.335.refs_0_), channel_id=1, source_target_pairs={{0,2},{1,3},{2,0},{3,1},{4,6},{5,7},{6,4},{7,5},{8,10},{9,11},{10,... | collective-permute-start | bytes 1572872 | tf_op jit(solution)/shard_map/ppermute | solution.py:74
  86.6 14.3 %collective-permute-start.15 = (bf16[256,1024]{1,0:T(8,128)(2,1)S(1)}, bf16[256,1024]{1,0:T(8,128)(2,1)S(1)}, u32[]{:S(2)}, u32[]{:S(2)}) collective-permute-start(bf16[256,1024]{1,0:T(8,128)(2,1)S(1)} %get-tuple-element.351.refs_0_), channel_id=1, source_target_pairs={{0,2},{1,3},{2,0},{3,1},{4,6},{5,7},{6,4},{7,5},{8,10},{9,11},{10,... | collective-permute-start | bytes 1572872 | tf_op jit(solution)/shard_map/ppermute | solution.py:74
  102.5 14.3 %collective-permute-start.16 = (bf16[256,1024]{1,0:T(8,128)(2,1)S(1)}, bf16[256,1024]{1,0:T(8,128)(2,1)S(1)}, u32[]{:S(2)}, u32[]{:S(2)}) collective-permute-start(bf16[256,1024]{1,0:T(8,128)(2,1)S(1)} %get-tuple-element.352.refs_0_), channel_id=1, source_target_pairs={{0,2},{1,3},{2,0},{3,1},{4,6},{5,7},{6,4},{7,5},{8,10},{9,11},{10,... | collective-permute-start | bytes 1572872 | tf_op jit(solution)/shard_map/ppermute | solution.py:74
  163.2 20.0 %collective-permute-start.29 = (bf16[256,1024]{1,0:T(8,128)(2,1)}, bf16[256,1024]{1,0:T(8,128)(2,1)S(1)}, u32[]{:S(2)}, u32[]{:S(2)}) collective-permute-start(bf16[256,1024]{1,0:T(8,128)(2,1)} %copy-done.116), channel_id=1, source_target_pairs={{0,2},{1,3},{2,0},{3,1},{4,6},{5,7},{6,4},{7,5},{8,10},{9,11},{10,... | collective-permute-start | bytes 1572872 | tf_op jit(solution)/shard_map/ppermute | solution.py:74
  201.5 14.7 %collective-permute-start.38 = (bf16[256,1024]{1,0:T(8,128)(2,1)}, bf16[256,1024]{1,0:T(8,128)(2,1)}, u32[]{:S(2)}, u32[]{:S(2)}) collective-permute-start(bf16[256,1024]{1,0:T(8,128)(2,1)} %get-tuple-element.446.refs_0_), channel_id=1, source_target_pairs={{0,2},{1,3},{2,0},{3,1},{4,6},{5,7},{6,4},{7,5},{8,10},{9,11},{10,... | collective-permute-start | bytes 1572872 | tf_op jit(solution)/shard_map/ppermute | solution.py:74
  235.5 35.3 %collective-permute-start.48 = (bf16[4,4,128,256]{3,2,1,0:T(8,128)(2,1)}, bf16[4,4,128,256]{3,2,1,0:T(8,128)(2,1)}, u32[]{:S(2)}, u32[]{:S(2)}) collective-permute-start(bf16[4,4,128,256]{3,2,1,0:T(8,128)(2,1)} %get-tuple-element.486), channel_id=1, source_target_pairs={{0,4},{4,0},{8,12},{12,8},{16,20},{20,16},{24,28},{28,24},{1,5},{5... | collective-permute-start | bytes 3145736 | tf_op jit(solution)/shard_map/ppermute | solution.py:1296
  250.3 34.2 %collective-permute-start.47 = (bf16[4,128,1024]{2,1,0:T(8,128)(2,1)}, bf16[4,128,1024]{2,1,0:T(8,128)(2,1)S(1)}, u32[]{:S(2)}, u32[]{:S(2)}) collective-permute-start(bf16[4,128,1024]{2,1,0:T(8,128)(2,1)} %get-tuple-element.482), channel_id=1, source_target_pairs={{0,4},{4,0},{8,12},{12,8},{16,20},{20,16},{24,28},{28,24},{1,5},{5... | collective-permute-start | bytes 3145736 | tf_op jit(solution)/shard_map/ppermute | solution.py:1296
  251.8 37.9 %collective-permute-start.52 = (bf16[4,128,1024]{2,1,0:T(8,128)(2,1)}, bf16[4,128,1024]{2,1,0:T(8,128)(2,1)S(1)}, u32[]{:S(2)}, u32[]{:S(2)}) collective-permute-start(bf16[4,128,1024]{2,1,0:T(8,128)(2,1)} %get-tuple-element.513), channel_id=1, source_target_pairs={{0,8},{4,12},{8,0},{12,4},{16,24},{20,28},{24,16},{28,20},{1,9},{5... | collective-permute-start | bytes 3145736 | tf_op jit(solution)/shard_map/ppermute | solution.py:1296
  270.2 17.1 %collective-permute-start.45 = (bf16[256,1024]{1,0:T(8,128)(2,1)S(1)}, bf16[256,1024]{1,0:T(8,128)(2,1)S(1)}, u32[]{:S(2)}, u32[]{:S(2)}) collective-permute-start(bf16[256,1024]{1,0:T(8,128)(2,1)S(1)} %get-tuple-element.478), channel_id=1, source_target_pairs={{0,1},{1,0},{2,3},{3,2},{4,5},{5,4},{6,7},{7,6},{8,9},{9,8},{10,11... | collective-permute-start | bytes 1572872 | tf_op jit(solution)/shard_map/ppermute | solution.py:69
  270.4 16.9 %collective-permute-start.46 = (bf16[256,1024]{1,0:T(8,128)(2,1)S(1)}, bf16[256,1024]{1,0:T(8,128)(2,1)S(1)}, u32[]{:S(2)}, u32[]{:S(2)}) collective-permute-start(bf16[256,1024]{1,0:T(8,128)(2,1)S(1)} %get-tuple-element.480), channel_id=1, source_target_pairs={{0,1},{1,0},{2,3},{3,2},{4,5},{5,4},{6,7},{7,6},{8,9},{9,8},{10,11... | collective-permute-start | bytes 1572872 | tf_op jit(solution)/shard_map/ppermute | solution.py:69
  273.2 30.2 %collective-permute-start.50 = (bf16[2,4,128,256]{3,2,1,0:T(8,128)(2,1)}, bf16[2,4,128,256]{3,2,1,0:T(8,128)(2,1)}, u32[]{:S(2)}, u32[]{:S(2)}) collective-permute-start(bf16[2,4,128,256]{3,2,1,0:T(8,128)(2,1)} %get-tuple-element.496), channel_id=1, source_target_pairs={{0,8},{4,12},{8,0},{12,4},{16,24},{20,28},{24,16},{28,20},{1,9},{5... | collective-permute-start | bytes 1572872 | tf_op jit(solution)/shard_map/ppermute | solution.py:1296
  285.7 20.3 %collective-permute-start.51 = (bf16[2,128,1024]{2,1,0:T(8,128)(2,1)}, bf16[2,128,1024]{2,1,0:T(8,128)(2,1)}, u32[]{:S(2)}, u32[]{:S(2)}) collective-permute-start(bf16[2,128,1024]{2,1,0:T(8,128)(2,1)} %get-tuple-element.498), channel_id=1, source_target_pairs={{0,8},{4,12},{8,0},{12,4},{16,24},{20,28},{24,16},{28,20},{1,9},{5... | collective-permute-start | bytes 1572872 | tf_op jit(solution)/shard_map/ppermute | solution.py:1296
  291.8 20.2 %collective-permute-start.49 = (bf16[256,1024]{1,0:T(8,128)(2,1)}, bf16[256,1024]{1,0:T(8,128)(2,1)}, u32[]{:S(2)}, u32[]{:S(2)}) collective-permute-start(bf16[256,1024]{1,0:T(8,128)(2,1)} %get-tuple-element.492), channel_id=1, source_target_pairs={{0,2},{1,3},{2,0},{3,1},{4,6},{5,7},{6,4},{7,5},{8,10},{9,11},{10,... | collective-permute-start | bytes 1572872 | tf_op jit(solution)/shard_map/ppermute | solution.py:74
  293.3 25.2 %collective-permute-start.57 = (bf16[2,128,1024]{2,1,0:T(8,128)(2,1)}, bf16[2,128,1024]{2,1,0:T(8,128)(2,1)}, u32[]{:S(2)}, u32[]{:S(2)}) collective-permute-start(bf16[2,128,1024]{2,1,0:T(8,128)(2,1)} %get-tuple-element.538), channel_id=1, source_target_pairs={{0,16},{4,20},{8,24},{12,28},{16,0},{20,4},{24,8},{28,12},{1,17},{... | collective-permute-start | bytes 1572872 | tf_op jit(solution)/shard_map/ppermute | solution.py:1296
  301.9 18.4 %collective-permute-start.56 = (bf16[4,2,128,256]{3,2,1,0:T(8,128)(2,1)}, bf16[4,2,128,256]{3,2,1,0:T(8,128)(2,1)S(1)}, u32[]{:S(2)}, u32[]{:S(2)}) collective-permute-start(bf16[4,2,128,256]{3,2,1,0:T(8,128)(2,1)} %get-tuple-element.536), channel_id=1, source_target_pairs={{0,4},{4,0},{8,12},{12,8},{16,20},{20,16},{24,28},{28,24},{1,5},{5... | collective-permute-start | bytes 1572872 | tf_op jit(solution)/shard_map/ppermute | solution.py:1296
  303.4 22.4 %collective-permute-start.59 = (bf16[4,2,128,256]{3,2,1,0:T(8,128)(2,1)}, bf16[4,2,128,256]{3,2,1,0:T(8,128)(2,1)S(1)}, u32[]{:S(2)}, u32[]{:S(2)}) collective-permute-start(bf16[4,2,128,256]{3,2,1,0:T(8,128)(2,1)} %get-tuple-element.545), channel_id=1, source_target_pairs={{0,4},{4,0},{8,12},{12,8},{16,20},{20,16},{24,28},{28,24},{1,5},{5... | collective-permute-start | bytes 1572872 | tf_op jit(solution)/shard_map/ppermute | solution.py:1296
  328.3 26.7 %collective-permute-start.67 = (bf16[1,128,1024]{2,1,0:T(8,128)(2,1)S(1)}, bf16[1,128,1024]{2,1,0:T(8,128)(2,1)S(1)}, u32[]{:S(2)}, u32[]{:S(2)}) collective-permute-start(bf16[1,128,1024]{2,1,0:T(8,128)(2,1)S(1)} %copy-done.119), channel_id=1, source_target_pairs={{0,16},{4,20},{8,24},{12,28},{16,0},{20,4},{24,8},{28,12},{1,17},{... | collective-permute-start | bytes 786440 | tf_op jit(solution)/shard_map/ppermute | solution.py:1296
  331.2 26.0 %collective-permute-start.66 = (bf16[1,128,1024]{2,1,0:T(8,128)(2,1)S(1)}, bf16[1,128,1024]{2,1,0:T(8,128)(2,1)S(1)}, u32[]{:S(2)}, u32[]{:S(2)}) collective-permute-start(bf16[1,128,1024]{2,1,0:T(8,128)(2,1)S(1)} %copy-done.120), channel_id=1, source_target_pairs={{0,4},{4,0},{8,12},{12,8},{16,20},{20,16},{24,28},{28,24},{1,5},{5... | collective-permute-start | bytes 786440 | tf_op jit(solution)/shard_map/ppermute | solution.py:1296
  332.2 28.5 %collective-permute-start.65 = (bf16[1,4,128,256]{3,2,1,0:T(8,128)(2,1)S(1)}, bf16[1,4,128,256]{3,2,1,0:T(8,128)(2,1)S(1)}, u32[]{:S(2)}, u32[]{:S(2)}) collective-permute-start(bf16[1,4,128,256]{3,2,1,0:T(8,128)(2,1)S(1)} %copy-done.118), channel_id=1, source_target_pairs={{0,16},{4,20},{8,24},{12,28},{16,0},{20,4},{24,8},{28,12},{1,17},{... | collective-permute-start | bytes 786440 | tf_op jit(solution)/shard_map/ppermute | solution.py:1296
  338.9 24.6 %collective-permute-start.63 = (bf16[1,2,128,256]{3,2,1,0:T(8,128)(2,1)}, bf16[1,2,128,256]{3,2,1,0:T(8,128)(2,1)S(1)}, u32[]{:S(2)}, u32[]{:S(2)}) collective-permute-start(bf16[1,2,128,256]{3,2,1,0:T(8,128)(2,1)} %get-tuple-element.561), channel_id=1, source_target_pairs={{0,16},{4,20},{8,24},{12,28},{16,0},{20,4},{24,8},{28,12},{1,17},{... | collective-permute-start | bytes 393224 | tf_op jit(solution)/shard_map/ppermute | solution.py:1296
  341.6 23.3 %collective-permute-start.64 = (bf16[1,2,128,256]{3,2,1,0:T(8,128)(2,1)}, bf16[1,2,128,256]{3,2,1,0:T(8,128)(2,1)S(1)}, u32[]{:S(2)}, u32[]{:S(2)}) collective-permute-start(bf16[1,2,128,256]{3,2,1,0:T(8,128)(2,1)} %get-tuple-element.563), channel_id=1, source_target_pairs={{0,16},{4,20},{8,24},{12,28},{16,0},{20,4},{24,8},{28,12},{1,17},{... | collective-permute-start | bytes 393224 | tf_op jit(solution)/shard_map/ppermute | solution.py:1296
  (166 other events, 1250.7 us)
Sparse Core Ops, SparseCore 0:
  162.7 89.5 reduce-scatter.1
where the time goes:
time: 378 us; the launch traced here: 373 us
  Pallas kernels  203 us (54%)
  waiting for transfers between devices  82.2 us (22%)
  starting transfers between devices  59.1 us (16%)
  between operations  16.4 us (4%)
  local copies, waits for them, and re-layouts  12.1 us (3%)
    pallas_call x92, Pallas kernels, __call__(): pl.pallas_call(body, grid=(1,), out_shape=[pltpu.HBM(o.shape, o.dtype) if...  203 us
    ppermute x17, waiting for transfers between devices, chip_swap(): return lax.ppermute(x, 'mp', [(i, i ^ 2) for i in range(size)])  44 us
    ppermute x18, waiting for transfers between devices, dp_swap(): return lax.ppermute(x, 'dp', [(i, i ^ stride) for i in range(size)])  33.7 us
    ppermute x17, starting transfers between devices, chip_swap(): return lax.ppermute(x, 'mp', [(i, i ^ 2) for i in range(size)])  28.4 us
    ppermute x18, starting transfers between devices, dp_swap(): return lax.ppermute(x, 'dp', [(i, i ^ stride) for i in range(size)])  24.1 us
    unnamed x244, local copies, waits for them, and re-layouts  11.3 us
  transfers between devices with their start and end apart: 69, of which 35 were waited for; matrix products, arithmetic and copies ran while one was open for 1% of the time, Pallas kernels for 51%

commit v1 on v0

--- a/solution.py
+++ b/solution.py
@@ -1560,11 +1560,11 @@
                 run, [parts_order(rising)] * 2, scal, normed, rows, in_low, mixed, True
             )
         else:
-            for x in mix_rest[1:]:
-                x.step()
             swapped = [core_swap(ends[i]) for i in both]
         filt_out, narrow = filter_bwd(run, layer, length, scal, taps_grad, pos, filter_weights, filt[layer][1])
         if layer == 0:
+            for x in mix_rest[1:]:
+                x.step()
             up_big.step()
             send, own, own_sums = last_pick(run, scal, ends[2:], swapped, entry)
             there = chip_swap(send)

time: 378 us -> 382 us (1.011)
  transfers between devices with their start and end apart: 69 -> 69, of which waited for: 35 -> 32; matrix products, arithmetic and copies ran while one was open for 1% -> 1% of each run, Pallas kernels for 51% -> 51%
where the time goes in v1:
time: 382 us; the launch traced here: 376 us
  Pallas kernels  203 us (53%)
  waiting for transfers between devices  83 us (22%)
  starting transfers between devices  61.7 us (16%)
  between operations  16.5 us (4%)
  local copies, waits for them, and re-layouts  12 us (3%)
    pallas_call x92, Pallas kernels, __call__(): pl.pallas_call(body, grid=(1,), out_shape=[pltpu.HBM(o.shape, o.dtype) if...  203 us
    ppermute x17, waiting for transfers between devices, chip_swap(): return lax.ppermute(x, 'mp', [(i, i ^ 2) for i in range(size)])  43.2 us
    ppermute x18, waiting for transfers between devices, dp_swap(): return lax.ppermute(x, 'dp', [(i, i ^ stride) for i in range(size)])  35.3 us
    ppermute x17, starting transfers between devices, chip_swap(): return lax.ppermute(x, 'mp', [(i, i ^ 2) for i in range(size)])  30.2 us
    ppermute x18, starting transfers between devices, dp_swap(): return lax.ppermute(x, 'dp', [(i, i ^ stride) for i in range(size)])  25 us
    unnamed x244, local copies, waits for them, and re-layouts  11.3 us
  transfers between devices with their start and end apart: 69, of which 32 were waited for; matrix products, arithmetic and copies ran while one was open for 1% of the time, Pallas kernels for 51%

profile of v1, /device:TPU:0, one launch (start us, length us, event | category | flops | bytes accessed | tf_op | source)
XLA Modules:
  0.0 376.4 jit_solution(6827317823412452393)
XLA Ops:
  12.4 8.2 %filter_fwd.2 = (f32[1792,256]{1,0:T(8,128)}, f32[6,64,896]{2,1,0:T(8,128)}, f32[8,128]{1,0:T(8,128)}) custom-call(s32[5]{0:T(128)S(1)} %stack.19.refs_0_, f32[64,896]{1,0:T(8,128)} %constant.52.clone.refs_1_.refs_2_, f32[2,33,64]{2,1,0:T(8,128)} %copy.58.refs_2_, f32[2,64]{1,0:T(2,128)} %refs_3_.25, f32[2,64]{1,0:T(2,128)} %refs_3_.41, ...), custom_call_target="tpu_custom_call" | custom-call | flops 1 | bytes 1 | tf_op jit(solution)/shard_map/filter_fwd/pallas_call | solution.py:161
  27.6 7.6 %mix_fwd.4 = (f32[512,768]{1,0:T(8,128)}, f32[512,256]{1,0:T(8,128)}, bf16[512,256]{1,0:T(8,128)(2,1)}, bf16[1792,512]{1,0:T(8,128)(2,1)S(1)}, f32[8,768]{1,0:T(...) custom-call(s32[5]{0:T(128)S(1)} %stack.19.refs_0_, ...), custom_call_target="tpu_custom_call" | custom-call | flops 1 | bytes 1 | tf_op jit(solution)/shard_map/mix_fwd/pallas_call | solution.py:161
  43.0 9.8 %mix_fwd.5 = (f32[512,768]{1,0:T(8,128)}, f32[512,256]{1,0:T(8,128)}, bf16[512,256]{1,0:T(8,128)(2,1)}, bf16[1792,512]{1,0:T(8,128)(2,1)}, f32[8,768]{1,0:T(8,12...) custom-call(s32[5]{0:T(128)S(1)} %stack.19.refs_0_, f32[3,2,256]{2,1,0:T(2,128)S(1)} %bitcast.31, ...), custom_call_target="tpu_custom_call" | custom-call | flops 1 | bytes 1 | tf_op jit(solution)/shard_map/mix_fwd/pallas_call | solution.py:161
  61.9 6.5 %filter_fwd.3 = (f32[1792,256]{1,0:T(8,128)}, f32[6,64,896]{2,1,0:T(8,128)}, f32[8,128]{1,0:T(8,128)}) custom-call(s32[5]{0:T(128)S(1)} %stack.19.refs_0_, f32[64,896]{1,0:T(8,128)S(1)} %copy-done.9, f32[2,33,64]{2,1,0:T(8,128)S(1)} %copy-done.72, f32[2,64]{1,0:T(2,128)S(1)} %copy-done.114, f32[2,64]{1,0:T(2,128)S(1)} %copy-done.103, ...), custom_call_target="tpu_custom_call" | custom-call | flops 1 | bytes 1 | tf_op jit(solution)/shard_map/filter_fwd/pallas_call | solution.py:161
  76.3 8.8 %collective-permute-done.10.refs_1_ = bf16[256,1024]{1,0:T(8,128)(2,1)S(1)} collective-permute-done((bf16[256,1024]{1,0:T(8,128)(2,1)S(1)}, bf16[256,1024]{1,0:T(8,128)(2,1)S(1)}, u32[]{:S(2)}, u32[]{:S(2)}) %collective-permute-start.10) | collective-permute-done | bytes 524320 | tf_op jit(solution)/shard_map/ppermute | solution.py:74
  88.8 7.5 %mix_fwd.6 = (f32[512,768]{1,0:T(8,128)}, f32[512,256]{1,0:T(8,128)}, bf16[512,256]{1,0:T(8,128)(2,1)}, bf16[1792,512]{1,0:T(8,128)(2,1)S(1)}, f32[8,768]{1,0:T(...) custom-call(s32[5]{0:T(128)S(1)} %stack.19.refs_0_, ...), custom_call_target="tpu_custom_call" | custom-call | flops 1 | bytes 1 | tf_op jit(solution)/shard_map/mix_fwd/pallas_call | solution.py:161
  96.5 4.5 %collective-permute-done.15.refs_1_ = bf16[256,1024]{1,0:T(8,128)(2,1)S(1)} collective-permute-done((bf16[256,1024]{1,0:T(8,128)(2,1)S(1)}, bf16[256,1024]{1,0:T(8,128)(2,1)S(1)}, u32[]{:S(2)}, u32[]{:S(2)}) %collective-permute-start.15) | collective-permute-done | bytes 524320 | tf_op jit(solution)/shard_map/ppermute | solution.py:74
  104.7 9.3 %mix_fwd.7 = (f32[512,768]{1,0:T(8,128)}, f32[512,256]{1,0:T(8,128)}, bf16[512,256]{1,0:T(8,128)(2,1)}, bf16[1792,512]{1,0:T(8,128)(2,1)}, f32[8,768]{1,0:T(8,12...) custom-call(s32[5]{0:T(128)S(1)} %stack.19.refs_0_, f32[3,2,256]{2,1,0:T(2,128)S(1)} %bitcast.33, ...), custom_call_target="tpu_custom_call" | custom-call | flops 1 | bytes 1 | tf_op jit(solution)/shard_map/mix_fwd/pallas_call | solution.py:161
  123.2 5.7 %ffn_bwd.4 = (bf16[512,1024]{1,0:T(8,128)(2,1)}, f32[1,1024]{1,0:T(1,128)}, bf16[256,1024]{1,0:T(8,128)(2,1)S(1)}, f32[256,1024]{1,0:T(8,128)S(1)}, f32[8,128]{1,0:T(8,128)}) custom-call(bf16[256,1024]{1,0:T(8,128)(2,1)S(1)} %get-tuple-element.370.refs_0_.refs_4_.refs_3_, bf16[256,1024]{1,0:T(8,128)(2,1)S(1)} %collective-permute-done.22.refs_1_.refs_5_, ...), custom_call_target="tpu_custom_call" | custom-call | flops 1 | bytes 1 | tf_op jit(solution)/shard_map/ffn_bwd/pallas_call | solution.py:161
  138.3 5.7 %ffn_bwd.5 = (bf16[512,1024]{1,0:T(8,128)(2,1)}, f32[1,1024]{1,0:T(1,128)}, bf16[256,1024]{1,0:T(8,128)(2,1)S(1)}, f32[256,1024]{1,0:T(8,128)S(1)}, f32[8,128]{1,0:T(8,128)}) custom-call(bf16[256,1024]{1,0:T(8,128)(2,1)S(1)} %get-tuple-element.383.refs_0_.refs_6_.refs_3_, bf16[256,1024]{1,0:T(8,128)(2,1)S(1)} %collective-permute-done.26.refs_1_.refs_7_, ...), custom_call_target="tpu_custom_call" | custom-call | flops 1 | bytes 1 | tf_op jit(solution)/shard_map/ffn_bwd/pallas_call | solution.py:161
  150.2 6.5 %ffn_whole.1 = (bf16[2,1024,1024]{2,1,0:T(8,128)(2,1)}, f32[8,128]{1,0:T(8,128)}) custom-call(bf16[256,1024]{1,0:T(8,128)(2,1)S(1)} %get-tuple-element.364.refs_0_, bf16[256,1024]{1,0:T(8,128)(2,1)S(1)} %collective-permute-done.19.refs_1_, bf16[256,1024]{1,0:T(8,128)(2,1)S(1)} %get-tuple-element.377.refs_0_.refs_2_, ...), custom_call_target="tpu_custom_call" | custom-call | flops 1 | bytes 1 | tf_op jit(solution)/shard_map/ffn_whole/pallas_call | solution.py:161
  166.2 16.3 %mix_bwd.2 = (bf16[1024,768]{1,0:T(8,128)(2,1)S(1)}, f32[896,256]{1,0:T(8,128)S(1)}, f32[16,256]{1,0:T(8,128)S(1)}, bf16[256,1024]{1,0:T(8,128)(2,1)S(1)}, bf16[...) custom-call(s32[5]{0:T(128)S(1)} %stack.19.refs_0_, ...), custom_call_target="tpu_custom_call" | custom-call | flops 1 | bytes 1 | tf_op jit(solution)/shard_map/mix_bwd/pallas_call | solution.py:161
  187.5 5.8 %mix_grad.2 = (bf16[4,4,128,256]{3,2,1,0:T(8,128)(2,1)}, bf16[4,4,128,256]{3,2,1,0:T(8,128)(2,1)}, f32[8,128]{1,0:T(8,128)}) custom-call(s32[5]{0:T(128)S(1)} %stack.19.refs_0_, bf16[256,1024]{1,0:T(8,128)(2,1)S(1)} %copy-done.17, bf16[256,1024]{1,0:T(8,128)(2,1)S(1)} %copy-done.20, bf16[256,1024]{1,0:T(8,128)(2,1)S(1)} %copy-done.19, ...), custom_call_target="tpu_custom_call" | custom-call | flops 1 | bytes 1 | tf_op jit(solution)/shard_map/mix_grad/pallas_call | solution.py:161
  203.8 7.4 %ffn_bwd.6 = (bf16[512,1024]{1,0:T(8,128)(2,1)}, f32[1,1024]{1,0:T(1,128)}, bf16[256,1024]{1,0:T(8,128)(2,1)S(1)}, f32[256,1024]{1,0:T(8,128)S(1)}, f32[8,128]{1,0:T(8,128)}) custom-call(bf16[256,1024]{1,0:T(8,128)(2,1)} %get-tuple-element.438.refs_0_.refs_5_, bf16[256,1024]{1,0:T(8,128)(2,1)} %collective-permute-done.36.refs_1_.refs_6_, ...), custom_call_target="tpu_custom_call" | custom-call | flops 1 | bytes 1 | tf_op jit(solution)/shard_map/ffn_bwd/pallas_call | solution.py:161
  211.4 4.8 %collective-permute-done.38.refs_1_ = bf16[256,1024]{1,0:T(8,128)(2,1)} collective-permute-done((bf16[256,1024]{1,0:T(8,128)(2,1)}, bf16[256,1024]{1,0:T(8,128)(2,1)}, u32[]{:S(2)}, u32[]{:S(2)}) %collective-permute-start.38) | collective-permute-done | bytes 524320 | tf_op jit(solution)/shard_map/ppermute | solution.py:74
  221.4 6.7 %ffn_bwd.7 = (bf16[512,1024]{1,0:T(8,128)(2,1)}, f32[1,1024]{1,0:T(1,128)}, bf16[256,1024]{1,0:T(8,128)(2,1)S(1)}, f32[256,1024]{1,0:T(8,128)S(1)}, f32[8,128]{1,0:T(8,128)}) custom-call(bf16[256,1024]{1,0:T(8,128)(2,1)S(1)} %get-tuple-element.451.refs_0_.refs_7_, bf16[256,1024]{1,0:T(8,128)(2,1)S(1)} %collective-permute-done.40.refs_1_.refs_8_, ...), custom_call_target="tpu_custom_call" | custom-call | flops 1 | bytes 1 | tf_op jit(solution)/shard_map/ffn_bwd/pallas_call | solution.py:161
  228.5 5.4 %collective-permute-done.39.refs_1_ = bf16[256,1024]{1,0:T(8,128)(2,1)S(1)} collective-permute-done((bf16[256,1024]{1,0:T(8,128)(2,1)S(1)}, bf16[256,1024]{1,0:T(8,128)(2,1)S(1)}, u32[]{:S(2)}, u32[]{:S(2)}) %collective-permute-start.39) | collective-permute-done | bytes 524320 | tf_op jit(solution)/shard_map/ppermute | solution.py:74
  238.3 7.7 %ffn_grad.1 = (bf16[4,128,1024]{2,1,0:T(8,128)(2,1)}, bf16[4,128,1024]{2,1,0:T(8,128)(2,1)}, bf16[4,128,1024]{2,1,0:T(8,128)(2,1)}, bf16[4,128,1024]{2,1,0:T(8,128)(2,1)}, f32[8,128]{1,0:T(8,128)}) custom-call(s32[5]{0:T(128)S(1)} %stack.19.refs_0_, bf16[256,1024]{1,0:T(8,128)(2,1)S(1)} %copy-done.32, bf16[256,1024]{1,0:T(8,128)(2,1)S(1)} %copy-done.34, ...), custom_call_target="tpu_custom_call" | custom-call | flops 1 | bytes 1 | tf_op jit(solution)/shard_map/ffn_grad/pallas_call | solution.py:161
  254.0 16.2 %mix_bwd.3 = (bf16[1024,768]{1,0:T(8,128)(2,1)S(1)}, f32[896,256]{1,0:T(8,128)S(1)}, f32[16,256]{1,0:T(8,128)S(1)}, bf16[256,1024]{1,0:T(8,128)(2,1)S(1)}, bf16[...) custom-call(s32[5]{0:T(128)S(1)} %stack.19.refs_0_, ...), custom_call_target="tpu_custom_call" | custom-call | flops 1 | bytes 1 | tf_op jit(solution)/shard_map/mix_bwd/pallas_call | solution.py:161
  277.9 6.7 %collective-permute-done.47.refs_1_ = bf16[4,128,1024]{2,1,0:T(8,128)(2,1)S(1)} collective-permute-done((bf16[4,128,1024]{2,1,0:T(8,128)(2,1)}, bf16[4,128,1024]{2,1,0:T(8,128)(2,1)S(1)}, u32[]{:S(2)}, u32[]{:S(2)}) %collective-permute-start.47) | collective-permute-done | bytes 1048608 | tf_op jit(solution)/shard_map/ppermute | solution.py:1296
  295.7 5.5 %mix_grad.3 = (bf16[4,2,128,256]{3,2,1,0:T(8,128)(2,1)}, bf16[4,2,128,256]{3,2,1,0:T(8,128)(2,1)}, bf16[4,2,128,256]{3,2,1,0:T(8,128)(2,1)}, bf16[4,2,128,256]{3,2,1,0:T(8,128)(2,1)}, f32[8,128]{1,0:T(8,128)}) custom-call(s32[5]{0:T(128)S(1)} %stack.19.refs_0_, bf16[256,1024]{1,0:T(8,128)(2,1)S(1)} %copy-done.10, bf16[256,1024]{1,0:T(8,128)(2,1)S(1)} %copy-done.12, ...), custom_call_target="tpu_custom_call" | custom-call | flops 1 | bytes 1 | tf_op jit(solution)/shard_map/mix_grad/pallas_call | solution.py:161
  303.9 6.0 %collective-permute-done.51.refs_1_ = bf16[2,128,1024]{2,1,0:T(8,128)(2,1)} collective-permute-done((bf16[2,128,1024]{2,1,0:T(8,128)(2,1)}, bf16[2,128,1024]{2,1,0:T(8,128)(2,1)}, u32[]{:S(2)}, u32[]{:S(2)}) %collective-permute-start.51) | collective-permute-done | bytes 524320 | tf_op jit(solution)/shard_map/ppermute | solution.py:1296
  338.9 4.1 %collective-permute-done.61.refs_1_ = bf16[2,2,128,256]{3,2,1,0:T(8,128)(2,1)S(1)} collective-permute-done((bf16[2,2,128,256]{3,2,1,0:T(8,128)(2,1)}, bf16[2,2,128,256]{3,2,1,0:T(8,128)(2,1)S(1)}, u32[]{:S(2)}, u32[]{:S(2)}) %collective-permute-start.61) | collective-permute-done | bytes 262176 | tf_op jit(solution)/shard_map/ppermute | solution.py:1296
  349.1 9.9 %collective-permute-done.67.refs_1_ = bf16[1,128,1024]{2,1,0:T(8,128)(2,1)S(1)} collective-permute-done((bf16[1,128,1024]{2,1,0:T(8,128)(2,1)S(1)}, bf16[1,128,1024]{2,1,0:T(8,128)(2,1)S(1)}, u32[]{:S(2)}, u32[]{:S(2)}) %collective-permute-start.67) | collective-permute-done | bytes 262176 | tf_op jit(solution)/shard_map/ppermute | solution.py:1296
  (458 shorter events, 177.4 us)
Async XLA Ops:
  7.2 351.8 %reduce-scatter.2.cloned.1.call-start = ((), (), s32[]{:S(2)}) async-start(), calls=%async_computation.1 | async-start | bytes 4718592 | tf_op jit(solution)/shard_map/reduce_scatter | solution.py:1505
  7.2 15.2 %collective-permute-start = (bf16[256,1024]{1,0:T(8,128)(2,1)}, bf16[256,1024]{1,0:T(8,128)(2,1)S(1)}, u32[]{:S(2)}, u32[]{:S(2)}) collective-permute-start(bf16[256,1024]{1,0:T(8,128)(2,1)} %bitcast.40), channel_id=1, source_target_pairs={{0,2},{1,3},{2,0},{3,1},{4,6},{5,7},{6,4},{7,5},{8,10},{9,11},{10,... | collective-permute-start | bytes 1572872 | tf_op jit(solution)/shard_map/ppermute | solution.py:74
  25.5 14.3 %collective-permute-start.3 = (bf16[256,1024]{1,0:T(8,128)(2,1)S(1)}, bf16[256,1024]{1,0:T(8,128)(2,1)S(1)}, u32[]{:S(2)}, u32[]{:S(2)}) collective-permute-start(bf16[256,1024]{1,0:T(8,128)(2,1)S(1)} %get-tuple-element.315.refs_1_), channel_id=1, source_target_pairs={{0,2},{1,3},{2,0},{3,1},{4,6},{5,7},{6,4},{7,5},{8,10},{9,11},{10,... | collective-permute-start | bytes 1572872 | tf_op jit(solution)/shard_map/ppermute | solution.py:74
  70.8 14.3 %collective-permute-start.10 = (bf16[256,1024]{1,0:T(8,128)(2,1)S(1)}, bf16[256,1024]{1,0:T(8,128)(2,1)S(1)}, u32[]{:S(2)}, u32[]{:S(2)}) collective-permute-start(bf16[256,1024]{1,0:T(8,128)(2,1)S(1)} %get-tuple-element.335.refs_0_), channel_id=1, source_target_pairs={{0,2},{1,3},{2,0},{3,1},{4,6},{5,7},{6,4},{7,5},{8,10},{9,11},{10,... | collective-permute-start | bytes 1572872 | tf_op jit(solution)/shard_map/ppermute | solution.py:74
  86.6 14.3 %collective-permute-start.15 = (bf16[256,1024]{1,0:T(8,128)(2,1)S(1)}, bf16[256,1024]{1,0:T(8,128)(2,1)S(1)}, u32[]{:S(2)}, u32[]{:S(2)}) collective-permute-start(bf16[256,1024]{1,0:T(8,128)(2,1)S(1)} %get-tuple-element.351.refs_0_), channel_id=1, source_target_pairs={{0,2},{1,3},{2,0},{3,1},{4,6},{5,7},{6,4},{7,5},{8,10},{9,11},{10,... | collective-permute-start | bytes 1572872 | tf_op jit(solution)/shard_map/ppermute | solution.py:74
  102.5 14.3 %collective-permute-start.16 = (bf16[256,1024]{1,0:T(8,128)(2,1)S(1)}, bf16[256,1024]{1,0:T(8,128)(2,1)S(1)}, u32[]{:S(2)}, u32[]{:S(2)}) collective-permute-start(bf16[256,1024]{1,0:T(8,128)(2,1)S(1)} %get-tuple-element.352.refs_0_), channel_id=1, source_target_pairs={{0,2},{1,3},{2,0},{3,1},{4,6},{5,7},{6,4},{7,5},{8,10},{9,11},{10,... | collective-permute-start | bytes 1572872 | tf_op jit(solution)/shard_map/ppermute | solution.py:74
  163.2 20.0 %collective-permute-start.29 = (bf16[256,1024]{1,0:T(8,128)(2,1)}, bf16[256,1024]{1,0:T(8,128)(2,1)S(1)}, u32[]{:S(2)}, u32[]{:S(2)}) collective-permute-start(bf16[256,1024]{1,0:T(8,128)(2,1)} %copy-done.116), channel_id=1, source_target_pairs={{0,2},{1,3},{2,0},{3,1},{4,6},{5,7},{6,4},{7,5},{8,10},{9,11},{10,... | collective-permute-start | bytes 1572872 | tf_op jit(solution)/shard_map/ppermute | solution.py:74
  201.5 14.7 %collective-permute-start.38 = (bf16[256,1024]{1,0:T(8,128)(2,1)}, bf16[256,1024]{1,0:T(8,128)(2,1)}, u32[]{:S(2)}, u32[]{:S(2)}) collective-permute-start(bf16[256,1024]{1,0:T(8,128)(2,1)} %get-tuple-element.446.refs_0_), channel_id=1, source_target_pairs={{0,2},{1,3},{2,0},{3,1},{4,6},{5,7},{6,4},{7,5},{8,10},{9,11},{10,... | collective-permute-start | bytes 1572872 | tf_op jit(solution)/shard_map/ppermute | solution.py:74
  235.5 38.3 %collective-permute-start.48 = (bf16[4,4,128,256]{3,2,1,0:T(8,128)(2,1)}, bf16[4,4,128,256]{3,2,1,0:T(8,128)(2,1)}, u32[]{:S(2)}, u32[]{:S(2)}) collective-permute-start(bf16[4,4,128,256]{3,2,1,0:T(8,128)(2,1)} %get-tuple-element.484), channel_id=1, source_target_pairs={{0,4},{4,0},{8,12},{12,8},{16,20},{20,16},{24,28},{28,24},{1,5},{5... | collective-permute-start | bytes 3145736 | tf_op jit(solution)/shard_map/ppermute | solution.py:1296
  250.3 34.2 %collective-permute-start.47 = (bf16[4,128,1024]{2,1,0:T(8,128)(2,1)}, bf16[4,128,1024]{2,1,0:T(8,128)(2,1)S(1)}, u32[]{:S(2)}, u32[]{:S(2)}) collective-permute-start(bf16[4,128,1024]{2,1,0:T(8,128)(2,1)} %get-tuple-element.482), channel_id=1, source_target_pairs={{0,4},{4,0},{8,12},{12,8},{16,20},{20,16},{24,28},{28,24},{1,5},{5... | collective-permute-start | bytes 3145736 | tf_op jit(solution)/shard_map/ppermute | solution.py:1296
  251.8 37.9 %collective-permute-start.52 = (bf16[4,128,1024]{2,1,0:T(8,128)(2,1)}, bf16[4,128,1024]{2,1,0:T(8,128)(2,1)S(1)}, u32[]{:S(2)}, u32[]{:S(2)}) collective-permute-start(bf16[4,128,1024]{2,1,0:T(8,128)(2,1)} %get-tuple-element.513), channel_id=1, source_target_pairs={{0,8},{4,12},{8,0},{12,4},{16,24},{20,28},{24,16},{28,20},{1,9},{5... | collective-permute-start | bytes 3145736 | tf_op jit(solution)/shard_map/ppermute | solution.py:1296
  270.2 17.1 %collective-permute-start.45 = (bf16[256,1024]{1,0:T(8,128)(2,1)S(1)}, bf16[256,1024]{1,0:T(8,128)(2,1)S(1)}, u32[]{:S(2)}, u32[]{:S(2)}) collective-permute-start(bf16[256,1024]{1,0:T(8,128)(2,1)S(1)} %get-tuple-element.478), channel_id=1, source_target_pairs={{0,1},{1,0},{2,3},{3,2},{4,5},{5,4},{6,7},{7,6},{8,9},{9,8},{10,11... | collective-permute-start | bytes 1572872 | tf_op jit(solution)/shard_map/ppermute | solution.py:69
  270.4 16.9 %collective-permute-start.46 = (bf16[256,1024]{1,0:T(8,128)(2,1)S(1)}, bf16[256,1024]{1,0:T(8,128)(2,1)S(1)}, u32[]{:S(2)}, u32[]{:S(2)}) collective-permute-start(bf16[256,1024]{1,0:T(8,128)(2,1)S(1)} %get-tuple-element.480), channel_id=1, source_target_pairs={{0,1},{1,0},{2,3},{3,2},{4,5},{5,4},{6,7},{7,6},{8,9},{9,8},{10,11... | collective-permute-start | bytes 1572872 | tf_op jit(solution)/shard_map/ppermute | solution.py:69
  276.2 27.1 %collective-permute-start.50 = (bf16[2,4,128,256]{3,2,1,0:T(8,128)(2,1)}, bf16[2,4,128,256]{3,2,1,0:T(8,128)(2,1)}, u32[]{:S(2)}, u32[]{:S(2)}) collective-permute-start(bf16[2,4,128,256]{3,2,1,0:T(8,128)(2,1)} %get-tuple-element.496), channel_id=1, source_target_pairs={{0,8},{4,12},{8,0},{12,4},{16,24},{20,28},{24,16},{28,20},{1,9},{5... | collective-permute-start | bytes 1572872 | tf_op jit(solution)/shard_map/ppermute | solution.py:1296
  285.7 24.2 %collective-permute-start.51 = (bf16[2,128,1024]{2,1,0:T(8,128)(2,1)}, bf16[2,128,1024]{2,1,0:T(8,128)(2,1)}, u32[]{:S(2)}, u32[]{:S(2)}) collective-permute-start(bf16[2,128,1024]{2,1,0:T(8,128)(2,1)} %get-tuple-element.498), channel_id=1, source_target_pairs={{0,8},{4,12},{8,0},{12,4},{16,24},{20,28},{24,16},{28,20},{1,9},{5... | collective-permute-start | bytes 1572872 | tf_op jit(solution)/shard_map/ppermute | solution.py:1296
  291.7 24.2 %collective-permute-start.49 = (bf16[256,1024]{1,0:T(8,128)(2,1)}, bf16[256,1024]{1,0:T(8,128)(2,1)}, u32[]{:S(2)}, u32[]{:S(2)}) collective-permute-start(bf16[256,1024]{1,0:T(8,128)(2,1)} %get-tuple-element.492), channel_id=1, source_target_pairs={{0,2},{1,3},{2,0},{3,1},{4,6},{5,7},{6,4},{7,5},{8,10},{9,11},{10,... | collective-permute-start | bytes 1572872 | tf_op jit(solution)/shard_map/ppermute | solution.py:74
  293.2 29.0 %collective-permute-start.57 = (bf16[2,128,1024]{2,1,0:T(8,128)(2,1)}, bf16[2,128,1024]{2,1,0:T(8,128)(2,1)}, u32[]{:S(2)}, u32[]{:S(2)}) collective-permute-start(bf16[2,128,1024]{2,1,0:T(8,128)(2,1)} %get-tuple-element.538), channel_id=1, source_target_pairs={{0,16},{4,20},{8,24},{12,28},{16,0},{20,4},{24,8},{28,12},{1,17},{... | collective-permute-start | bytes 1572872 | tf_op jit(solution)/shard_map/ppermute | solution.py:1296
  301.9 22.3 %collective-permute-start.56 = (bf16[4,2,128,256]{3,2,1,0:T(8,128)(2,1)}, bf16[4,2,128,256]{3,2,1,0:T(8,128)(2,1)S(1)}, u32[]{:S(2)}, u32[]{:S(2)}) collective-permute-start(bf16[4,2,128,256]{3,2,1,0:T(8,128)(2,1)} %get-tuple-element.536), channel_id=1, source_target_pairs={{0,4},{4,0},{8,12},{12,8},{16,20},{20,16},{24,28},{28,24},{1,5},{5... | collective-permute-start | bytes 1572872 | tf_op jit(solution)/shard_map/ppermute | solution.py:1296
  303.4 25.2 %collective-permute-start.59 = (bf16[4,2,128,256]{3,2,1,0:T(8,128)(2,1)}, bf16[4,2,128,256]{3,2,1,0:T(8,128)(2,1)S(1)}, u32[]{:S(2)}, u32[]{:S(2)}) collective-permute-start(bf16[4,2,128,256]{3,2,1,0:T(8,128)(2,1)} %get-tuple-element.545), channel_id=1, source_target_pairs={{0,4},{4,0},{8,12},{12,8},{16,20},{20,16},{24,28},{28,24},{1,5},{5... | collective-permute-start | bytes 1572872 | tf_op jit(solution)/shard_map/ppermute | solution.py:1296
  332.3 26.7 %collective-permute-start.67 = (bf16[1,128,1024]{2,1,0:T(8,128)(2,1)S(1)}, bf16[1,128,1024]{2,1,0:T(8,128)(2,1)S(1)}, u32[]{:S(2)}, u32[]{:S(2)}) collective-permute-start(bf16[1,128,1024]{2,1,0:T(8,128)(2,1)S(1)} %copy-done.119), channel_id=1, source_target_pairs={{0,16},{4,20},{8,24},{12,28},{16,0},{20,4},{24,8},{28,12},{1,17},{... | collective-permute-start | bytes 786440 | tf_op jit(solution)/shard_map/ppermute | solution.py:1296
  335.1 26.0 %collective-permute-start.66 = (bf16[1,128,1024]{2,1,0:T(8,128)(2,1)S(1)}, bf16[1,128,1024]{2,1,0:T(8,128)(2,1)S(1)}, u32[]{:S(2)}, u32[]{:S(2)}) collective-permute-start(bf16[1,128,1024]{2,1,0:T(8,128)(2,1)S(1)} %copy-done.120), channel_id=1, source_target_pairs={{0,4},{4,0},{8,12},{12,8},{16,20},{20,16},{24,28},{28,24},{1,5},{5... | collective-permute-start | bytes 786440 | tf_op jit(solution)/shard_map/ppermute | solution.py:1296
  335.3 29.3 %collective-permute-start.65 = (bf16[1,4,128,256]{3,2,1,0:T(8,128)(2,1)S(1)}, bf16[1,4,128,256]{3,2,1,0:T(8,128)(2,1)S(1)}, u32[]{:S(2)}, u32[]{:S(2)}) collective-permute-start(bf16[1,4,128,256]{3,2,1,0:T(8,128)(2,1)S(1)} %copy-done.118), channel_id=1, source_target_pairs={{0,16},{4,20},{8,24},{12,28},{16,0},{20,4},{24,8},{28,12},{1,17},{... | collective-permute-start | bytes 786440 | tf_op jit(solution)/shard_map/ppermute | solution.py:1296
  342.9 23.9 %collective-permute-start.63 = (bf16[1,2,128,256]{3,2,1,0:T(8,128)(2,1)}, bf16[1,2,128,256]{3,2,1,0:T(8,128)(2,1)S(1)}, u32[]{:S(2)}, u32[]{:S(2)}) collective-permute-start(bf16[1,2,128,256]{3,2,1,0:T(8,128)(2,1)} %get-tuple-element.561), channel_id=1, source_target_pairs={{0,16},{4,20},{8,24},{12,28},{16,0},{20,4},{24,8},{28,12},{1,17},{... | collective-permute-start | bytes 393224 | tf_op jit(solution)/shard_map/ppermute | solution.py:1296
  344.7 23.6 %collective-permute-start.64 = (bf16[1,2,128,256]{3,2,1,0:T(8,128)(2,1)}, bf16[1,2,128,256]{3,2,1,0:T(8,128)(2,1)S(1)}, u32[]{:S(2)}, u32[]{:S(2)}) collective-permute-start(bf16[1,2,128,256]{3,2,1,0:T(8,128)(2,1)} %get-tuple-element.563), channel_id=1, source_target_pairs={{0,16},{4,20},{8,24},{12,28},{16,0},{20,4},{24,8},{28,12},{1,17},{... | collective-permute-start | bytes 393224 | tf_op jit(solution)/shard_map/ppermute | solution.py:1296
  (166 other events, 1302.5 us)
Sparse Core Ops, SparseCore 0:
  162.7 89.5 reduce-scatter.1
